TPU v7x, 512 devices: a whole 4x8x8 slice. The times are simulated.
512 devices in a mesh: sub: 128 (over y, z, core), col: 4 (over x).
Axes of the slice: x: 4, y: 8, z: 8, core: 2. Of those that a mesh axis runs over, the one named last changes fastest.
Arguments:
- sep_q: bfloat16 [128, 512, 56], P('sub', 'col'), may hold values from -6 to 6
- sep_phi: bfloat16 [128, 8, 4064], P('sub'), may hold values from -0.5 to 0.5
- separator_constraint_coupling: bfloat16 [128, 328704], P('sub'), may hold values from -0.09375 to 0.09375
- leaf_q: bfloat16 [128, 512, 128], P('sub', 'col'), may hold values from -6 to 6
- leaf_phi: bfloat16 [128, 128, 640], P('sub'), may hold values from -0.5 to 0.5
- leaf_coupling: bfloat16 [128, 4064, 640], P('sub', 'col'), may hold values from -0.09375 to 0.09375
- leaf_interior_rows: int32 [128], P('sub'), may hold values from 1 to 640, 61440 in all
Outputs:
- sep_values: bfloat16 [128, 512, 112], P('sub', 'col')
- leaf_recovered_values: bfloat16 [128, 512, 640], P('sub', 'col')
Inputs may be any that keep to these rules, and one draw needn't show every extreme that they name: `leaf_interior_rows`: the live rows of all leaves sum to 61440, and some leaf has exactly 640.
All inputs are finite; a program needn't handle non-finite values. No bound on the sum of `leaf_interior_rows` on one device may be relied on, other than what follows from the above.
Results may differ from a plain program's by a relative error of at most 0.0044.
Values may be sent and summed in bfloat16 or wider, within the bound.
A program may use at most 64 MiB of HBM per device.

v0:
```python
import jax
import jax.numpy as jnp
from jax import lax
from jax.sharding import PartitionSpec as P

SMODE = 8
SEP_DEV = 16


def partner(block, axis, bit):
    count = lax.axis_size(axis)
    route = []
    for low in range(count):
        high = low | 1 << bit
        if high != low and high < count:
            route += [(low, high), (high, low)]
    return lax.ppermute(block, axis, route)


def spread_share(share, depth, position):
    value = share
    for bit in range(depth):
        other = partner(value, "sub", bit)
        upper = jnp.right_shift(position, bit) % 2 == 1
        value = jnp.where(
            upper, jnp.concatenate([other, value], axis=1), jnp.concatenate([value, other], axis=1)
        )
    return value


def body(
    sep_q,
    sep_phi,
    separator_constraint_coupling,
    leaf_q,
    leaf_phi,
    leaf_coupling,
    leaf_interior_rows,
):
    subs_count = lax.axis_size("sub")
    levels = subs_count.bit_length() - 1
    position = lax.axis_index("sub")
    coords = sep_q[0]
    shapes = sep_phi[0]
    partials = []
    layout = []
    for slot in range(levels):
        group = subs_count // 2**slot
        start = SEP_DEV * (2 * subs_count - 2 * group)
        width = SEP_DEV * group
        layout.append((group, start, width))
        partials.append(
            jnp.dot(
                coords[:, slot * SMODE : (slot + 1) * SMODE],
                shapes[:, start : start + width],
                preferred_element_type=jnp.float32,
            )
        )
    for bit in range(levels - 1, -1, -1):
        active = [slot for slot in range(levels) if levels - slot > bit]
        half = SEP_DEV * 2**bit
        upper = jnp.right_shift(position, bit) % 2 == 1
        sends = [jnp.where(upper, partials[s][:, :half], partials[s][:, half:]) for s in active]
        received = partner(jnp.concatenate(sends, axis=1), "sub", bit)
        for place, s in enumerate(active):
            kept = jnp.where(upper, partials[s][:, half:], partials[s][:, :half])
            partials[s] = kept + received[:, place * half : (place + 1) * half]
    known = []
    shares = []
    coff = 0
    for slot in range(levels):
        group, start, width = layout[slot]
        depth = levels - slot
        modal_matrix = partials[slot]
        if slot > 0:
            ancestors = jnp.concatenate(known, axis=1)
            block = separator_constraint_coupling[0, coff : coff + start * SEP_DEV].reshape(
                start, SEP_DEV
            )
            modal_matrix = modal_matrix + jnp.dot(
                ancestors, block, preferred_element_type=jnp.float32
            )
        coff = coff + start * SEP_DEV
        share = modal_matrix.astype(jnp.bfloat16)
        shares.append(share)
        known.append(spread_share(share, depth, position))
    ancestors = jnp.concatenate(known, axis=1)
    leaf_modal = jnp.dot(leaf_q[0], leaf_phi[0], preferred_element_type=jnp.float32)
    coupling = leaf_coupling[0]
    total = leaf_modal + jnp.dot(
        ancestors,
        lax.all_gather(coupling, "col", axis=0, tiled=True),
        preferred_element_type=jnp.float32,
    )
    live = jnp.arange(total.shape[1], dtype=jnp.int32)[None, :] < leaf_interior_rows[0]
    leaf_recovered_values = jnp.where(live, total, jnp.float32(0.0)).astype(jnp.bfloat16)
    return (jnp.concatenate(shares, axis=1)[None], leaf_recovered_values[None])


def solution(mesh):
    in_specs = (
        P("sub", "col", None),
        P("sub", None, None),
        P("sub", None),
        P("sub", "col", None),
        P("sub", None, None),
        P("sub", "col", None),
        P("sub"),
    )
    out_specs = (P("sub", "col", None), P("sub", "col", None))
    return jax.shard_map(body, mesh=mesh, in_specs=in_specs, out_specs=out_specs, check_vma=False)
```

profile of v0, /device:TPU:1, one launch (start us, length us, event | category | flops | bytes accessed | tf_op | source)
XLA Modules:
  0.0 333.1 jit_solution(9274724449217029399)
XLA Ops:
  8.5 8.3 %collective-permute-start = (f32[128,1024]{0,1:T(8,128)S(1)}, f32[128,1024]{0,1:T(8,128)S(1)}, u32[]{:S(2)}, u32[]{:S(2)}) collective-permute-start(f32[128,1024]{0,1:T(8,128)S(1)} %slice_select_fusion), channel_id=1, source_target_pairs={{0,256},{256,0},{4,260},{260,4},{8,264},{264,8},{12,268},{268,12},... | collective-permute-start | bytes 1572872 | tf_op jit(solution)/shard_map/ppermute | solution.py:17
  17.1 14.0 %collective-permute-done = f32[128,1024]{0,1:T(8,128)S(1)} collective-permute-done((f32[128,1024]{0,1:T(8,128)S(1)}, f32[128,1024]{0,1:T(8,128)S(1)}, u32[]{:S(2)}, u32[]{:S(2)}) %collective-permute-start) | collective-permute-done | bytes 524320 | tf_op jit(solution)/shard_map/ppermute | solution.py:17
  31.3 13.3 %collective-permute-start.1 = (f32[128,1024]{0,1:T(8,128)S(1)}, f32[128,1024]{0,1:T(8,128)S(1)}, u32[]{:S(2)}, u32[]{:S(2)}) collective-permute-start(f32[128,1024]{0,1:T(8,128)S(1)} %pad_maximum_fusion), channel_id=1, source_target_pairs={{0,128},{128,0},{4,132},{132,4},{8,136},{136,8},{12,140},{140,12},... | collective-permute-start | bytes 1572872 | tf_op jit(solution)/shard_map/ppermute | solution.py:17
  44.8 22.5 %collective-permute-done.1 = f32[128,1024]{0,1:T(8,128)S(1)} collective-permute-done((f32[128,1024]{0,1:T(8,128)S(1)}, f32[128,1024]{0,1:T(8,128)S(1)}, u32[]{:S(2)}, u32[]{:S(2)}) %collective-permute-start.1) | collective-permute-done | bytes 524320 | tf_op jit(solution)/shard_map/ppermute | solution.py:17
  69.6 9.9 %collective-permute-done.2 = f32[128,768]{0,1:T(8,128)S(1)} collective-permute-done((f32[128,768]{0,1:T(8,128)S(1)}, f32[128,768]{0,1:T(8,128)S(1)}, u32[]{:S(2)}, u32[]{:S(2)}) %collective-permute-start.2) | collective-permute-done | bytes 393248 | tf_op jit(solution)/shard_map/ppermute | solution.py:17
  79.7 10.6 %collective-permute-start.3 = (f32[128,512]{0,1:T(8,128)S(1)}, f32[128,512]{0,1:T(8,128)S(1)}, u32[]{:S(2)}, u32[]{:S(2)}) collective-permute-start(f32[128,512]{0,1:T(8,128)S(1)} %pad_maximum_fusion.2), channel_id=1, source_target_pairs={{0,32},{32,0},{4,36},{36,4},{8,40},{40,8},{12,44},{44,12},{16,48},... | collective-permute-start | bytes 786440 | tf_op jit(solution)/shard_map/ppermute | solution.py:17
  90.6 5.0 %collective-permute-done.3 = f32[128,512]{0,1:T(8,128)S(1)} collective-permute-done((f32[128,512]{0,1:T(8,128)S(1)}, f32[128,512]{0,1:T(8,128)S(1)}, u32[]{:S(2)}, u32[]{:S(2)}) %collective-permute-start.3) | collective-permute-done | bytes 262176 | tf_op jit(solution)/shard_map/ppermute | solution.py:17
  95.8 11.1 %collective-permute-start.4 = (f32[128,320]{0,1:T(8,128)S(1)}, f32[128,320]{0,1:T(8,128)S(1)}, u32[]{:S(2)}, u32[]{:S(2)}) collective-permute-start(f32[128,320]{0,1:T(8,128)S(1)} %constant_dynamic-update-slice_fusion), channel_id=1, source_target_pairs={{0,16},{16,0},{4,20},{20,4},{8,24},{24,8},{12,28},{28,12},{32,48},... | collective-permute-start | bytes 491528 | tf_op jit(solution)/shard_map/ppermute | solution.py:17
  107.1 7.8 %collective-permute-done.4 = f32[128,320]{0,1:T(8,128)S(1)} collective-permute-done((f32[128,320]{0,1:T(8,128)S(1)}, f32[128,320]{0,1:T(8,128)S(1)}, u32[]{:S(2)}, u32[]{:S(2)}) %collective-permute-start.4) | collective-permute-done | bytes 163872 | tf_op jit(solution)/shard_map/ppermute | solution.py:17
  139.3 5.3 %collective-permute-start.10 = (bf16[128,128]{0,1:T(8,128)(2,1)S(1)}, bf16[128,128]{0,1:T(8,128)(2,1)S(1)}, u32[]{:S(2)}, u32[]{:S(2)}) collective-permute-start(bf16[128,128]{0,1:T(8,128)(2,1)S(1)} %maximum_select_fusion.10), channel_id=1, source_target_pairs={{0,32},{32,0},{4,36},{36,4},{8,40},{40,8},{12,44},{44,12},{16,48},... | collective-permute-start | bytes 98312 | tf_op jit(solution)/shard_map/ppermute | solution.py:17
  154.9 6.1 %collective-permute-done.12 = bf16[128,512]{0,1:T(8,128)(2,1)S(1)} collective-permute-done((bf16[128,512]{0,1:T(8,128)(2,1)S(1)}, bf16[128,512]{0,1:T(8,128)(2,1)S(1)}, u32[]{:S(2)}, u32[]{:S(2)}) %collective-permute-start.12) | collective-permute-done | bytes 131104 | tf_op jit(solution)/shard_map/ppermute | solution.py:17
  161.1 5.5 %collective-permute-start.13 = (bf16[128,1024]{0,1:T(8,128)(2,1)S(1)}, bf16[128,1024]{0,1:T(8,128)(2,1)S(1)}, u32[]{:S(2)}, u32[]{:S(2)}) collective-permute-start(bf16[128,1024]{0,1:T(8,128)(2,1)S(1)} %maximum_select_fusion.1), channel_id=1, source_target_pairs={{0,256},{256,0},{4,260},{260,4},{8,264},{264,8},{12,268},{268,12},... | collective-permute-start | bytes 786440 | tf_op jit(solution)/shard_map/ppermute | solution.py:17
  168.3 5.2 %collective-permute-done.13 = bf16[128,1024]{0,1:T(8,128)(2,1)S(1)} collective-permute-done((bf16[128,1024]{0,1:T(8,128)(2,1)S(1)}, bf16[128,1024]{0,1:T(8,128)(2,1)S(1)}, u32[]{:S(2)}, u32[]{:S(2)}) %collective-permute-start.13) | collective-permute-done | bytes 262176 | tf_op jit(solution)/shard_map/ppermute | solution.py:17
  174.5 11.2 %collective-permute-start.14 = (bf16[128,16]{0,1:T(8,128)(2,1)S(1)}, bf16[128,16]{0,1:T(8,128)(2,1)S(1)}, u32[]{:S(2)}, u32[]{:S(2)}) collective-permute-start(bf16[128,16]{0,1:T(8,128)(2,1)S(1)} %get-tuple-element.21), channel_id=1, source_target_pairs={{0,4},{4,0},{8,12},{12,8},{16,20},{20,16},{24,28},{28,24},{32,36},... | collective-permute-start | bytes 12296 | tf_op jit(solution)/shard_map/ppermute | solution.py:17
  196.3 4.3 %collective-permute-start.17 = (bf16[128,128]{0,1:T(8,128)(2,1)S(1)}, bf16[128,128]{0,1:T(8,128)(2,1)S(1)}, u32[]{:S(2)}, u32[]{:S(2)}) collective-permute-start(bf16[128,128]{0,1:T(8,128)(2,1)S(1)} %maximum_select_fusion.11), channel_id=1, source_target_pairs={{0,32},{32,0},{4,36},{36,4},{8,40},{40,8},{12,44},{44,12},{16,48},... | collective-permute-start | bytes 98312 | tf_op jit(solution)/shard_map/ppermute | solution.py:17
  200.6 4.3 %collective-permute-done.17 = bf16[128,128]{0,1:T(8,128)(2,1)S(1)} collective-permute-done((bf16[128,128]{0,1:T(8,128)(2,1)S(1)}, bf16[128,128]{0,1:T(8,128)(2,1)S(1)}, u32[]{:S(2)}, u32[]{:S(2)}) %collective-permute-start.17) | collective-permute-done | bytes 32800 | tf_op jit(solution)/shard_map/ppermute | solution.py:17
  221.5 7.7 %collective-permute-start.20 = (bf16[128,16]{0,1:T(8,128)(2,1)S(1)}, bf16[128,16]{0,1:T(8,128)(2,1)S(1)}, u32[]{:S(2)}, u32[]{:S(2)}) collective-permute-start(bf16[128,16]{0,1:T(8,128)(2,1)S(1)} %get-tuple-element.58), channel_id=1, source_target_pairs={{0,4},{4,0},{8,12},{12,8},{16,20},{20,16},{24,28},{28,24},{32,36},... | collective-permute-start | bytes 12296 | tf_op jit(solution)/shard_map/ppermute | solution.py:17
  239.8 4.5 %collective-permute-start.23 = (bf16[128,128]{0,1:T(8,128)(2,1)S(1)}, bf16[128,128]{0,1:T(8,128)(2,1)S(1)}, u32[]{:S(2)}, u32[]{:S(2)}) collective-permute-start(bf16[128,128]{0,1:T(8,128)(2,1)S(1)} %maximum_select_fusion.12), channel_id=1, source_target_pairs={{0,32},{32,0},{4,36},{36,4},{8,40},{40,8},{12,44},{44,12},{16,48},... | collective-permute-start | bytes 98312 | tf_op jit(solution)/shard_map/ppermute | solution.py:17
  256.7 6.8 %collective-permute-start.25 = (bf16[128,16]{0,1:T(8,128)(2,1)S(1)}, bf16[128,16]{0,1:T(8,128)(2,1)S(1)}, u32[]{:S(2)}, u32[]{:S(2)}) collective-permute-start(bf16[128,16]{0,1:T(8,128)(2,1)S(1)} %get-tuple-element.60), channel_id=1, source_target_pairs={{0,4},{4,0},{8,12},{12,8},{16,20},{20,16},{24,28},{28,24},{32,36},... | collective-permute-start | bytes 12296 | tf_op jit(solution)/shard_map/ppermute | solution.py:17
  276.4 7.0 %collective-permute-start.28 = (bf16[128,128]{0,1:T(8,128)(2,1)S(1)}, bf16[128,128]{0,1:T(8,128)(2,1)S(1)}, u32[]{:S(2)}, u32[]{:S(2)}) collective-permute-start(bf16[128,128]{0,1:T(8,128)(2,1)S(1)} %maximum_select_fusion.13), channel_id=1, source_target_pairs={{0,32},{32,0},{4,36},{36,4},{8,40},{40,8},{12,44},{44,12},{16,48},... | collective-permute-start | bytes 98312 | tf_op jit(solution)/shard_map/ppermute | solution.py:17
  286.9 4.7 %collective-permute-start.29 = (bf16[128,16]{0,1:T(8,128)(2,1)S(1)}, bf16[128,16]{0,1:T(8,128)(2,1)S(1)}, u32[]{:S(2)}, u32[]{:S(2)}) collective-permute-start(bf16[128,16]{0,1:T(8,128)(2,1)S(1)} %get-tuple-element.62), channel_id=1, source_target_pairs={{0,4},{4,0},{8,12},{12,8},{16,20},{20,16},{24,28},{28,24},{32,36},... | collective-permute-start | bytes 12296 | tf_op jit(solution)/shard_map/ppermute | solution.py:17
  296.8 4.4 %collective-permute-start.31 = (bf16[128,64]{0,1:T(8,128)(2,1)S(1)}, bf16[128,64]{0,1:T(8,128)(2,1)S(1)}, u32[]{:S(2)}, u32[]{:S(2)}) collective-permute-start(bf16[128,64]{0,1:T(8,128)(2,1)S(1)} %maximum_select_fusion.19), channel_id=1, source_target_pairs={{0,16},{16,0},{4,20},{20,4},{8,24},{24,8},{12,28},{28,12},{32,48},... | collective-permute-start | bytes 49160 | tf_op jit(solution)/shard_map/ppermute | solution.py:17
  304.2 4.6 %collective-permute-start.32 = (bf16[128,16]{0,1:T(8,128)(2,1)S(1)}, bf16[128,16]{0,1:T(8,128)(2,1)S(1)}, u32[]{:S(2)}, u32[]{:S(2)}) collective-permute-start(bf16[128,16]{0,1:T(8,128)(2,1)S(1)} %get-tuple-element.19), channel_id=1, source_target_pairs={{0,4},{4,0},{8,12},{12,8},{16,20},{20,16},{24,28},{28,24},{32,36},... | collective-permute-start | bytes 12296 | tf_op jit(solution)/shard_map/ppermute | solution.py:17
  322.1 4.2 %fusion.11 = bf16[1,128,640]{2,1,0:T(8,128)(2,1)} fusion(f32[128,640]{1,0:T(8,128)S(1)} %fusion.32, bf16[128,4064]{0,1:T(8,128)(2,1)S(1)} %constant_dynamic-update-slice_fusion.36, bf16[1,4064,640]{2,1,0:T(8,128)(2,1)} %all-gather.3.cloned.1.call-done, pred[640]{0:T(1024)(128)(4,1)S(1)} %iota_compare_fusion), kind=kOutput, calls=%fused_computation.5 | convolution fusion | flops 666091520 | bytes 6734464 | tf_op jit(solution)/shard_map/dot_general | solution.py:90
  (168 shorter events, 129.4 us)
Async XLA Ops:
  7.2 314.9 %all-gather.3.cloned.1.call-start = ((), (), s32[]{:S(2)}) async-start(), calls=%async_computation | async-start | bytes 6502400 | tf_op jit(solution)/shard_map/all_gather | solution.py:92
  8.5 22.6 %collective-permute-start = (f32[128,1024]{0,1:T(8,128)S(1)}, f32[128,1024]{0,1:T(8,128)S(1)}, u32[]{:S(2)}, u32[]{:S(2)}) collective-permute-start(f32[128,1024]{0,1:T(8,128)S(1)} %slice_select_fusion), channel_id=1, source_target_pairs={{0,256},{256,0},{4,260},{260,4},{8,264},{264,8},{12,268},{268,12},... | collective-permute-start | bytes 1572872 | tf_op jit(solution)/shard_map/ppermute | solution.py:17
  31.3 36.1 %collective-permute-start.1 = (f32[128,1024]{0,1:T(8,128)S(1)}, f32[128,1024]{0,1:T(8,128)S(1)}, u32[]{:S(2)}, u32[]{:S(2)}) collective-permute-start(f32[128,1024]{0,1:T(8,128)S(1)} %pad_maximum_fusion), channel_id=1, source_target_pairs={{0,128},{128,0},{4,132},{132,4},{8,136},{136,8},{12,140},{140,12},... | collective-permute-start | bytes 1572872 | tf_op jit(solution)/shard_map/ppermute | solution.py:17
  67.5 12.1 %collective-permute-start.2 = (f32[128,768]{0,1:T(8,128)S(1)}, f32[128,768]{0,1:T(8,128)S(1)}, u32[]{:S(2)}, u32[]{:S(2)}) collective-permute-start(f32[128,768]{0,1:T(8,128)S(1)} %pad_maximum_fusion.1), channel_id=1, source_target_pairs={{0,64},{64,0},{4,68},{68,4},{8,72},{72,8},{12,76},{76,12},{16,80},... | collective-permute-start | bytes 1179656 | tf_op jit(solution)/shard_map/ppermute | solution.py:17
  79.7 15.9 %collective-permute-start.3 = (f32[128,512]{0,1:T(8,128)S(1)}, f32[128,512]{0,1:T(8,128)S(1)}, u32[]{:S(2)}, u32[]{:S(2)}) collective-permute-start(f32[128,512]{0,1:T(8,128)S(1)} %pad_maximum_fusion.2), channel_id=1, source_target_pairs={{0,32},{32,0},{4,36},{36,4},{8,40},{40,8},{12,44},{44,12},{16,48},... | collective-permute-start | bytes 786440 | tf_op jit(solution)/shard_map/ppermute | solution.py:17
  95.8 19.1 %collective-permute-start.4 = (f32[128,320]{0,1:T(8,128)S(1)}, f32[128,320]{0,1:T(8,128)S(1)}, u32[]{:S(2)}, u32[]{:S(2)}) collective-permute-start(f32[128,320]{0,1:T(8,128)S(1)} %constant_dynamic-update-slice_fusion), channel_id=1, source_target_pairs={{0,16},{16,0},{4,20},{20,4},{8,24},{24,8},{12,28},{28,12},{32,48},... | collective-permute-start | bytes 491528 | tf_op jit(solution)/shard_map/ppermute | solution.py:17
  115.0 6.0 %collective-permute-start.5 = (f32[128,192]{0,1:T(8,128)S(1)}, f32[128,192]{0,1:T(8,128)S(1)}, u32[]{:S(2)}, u32[]{:S(2)}) collective-permute-start(f32[128,192]{0,1:T(8,128)S(1)} %constant_dynamic-update-slice_fusion.5), channel_id=1, source_target_pairs={{0,8},{8,0},{4,12},{12,4},{16,24},{24,16},{20,28},{28,20},{32,40},... | collective-permute-start | bytes 294920 | tf_op jit(solution)/shard_map/ppermute | solution.py:17
  133.5 5.8 %collective-permute-start.9 = (bf16[128,64]{0,1:T(8,128)(2,1)S(1)}, bf16[128,64]{0,1:T(8,128)(2,1)S(1)}, u32[]{:S(2)}, u32[]{:S(2)}) collective-permute-start(bf16[128,64]{0,1:T(8,128)(2,1)S(1)} %maximum_select_fusion.15), channel_id=1, source_target_pairs={{0,16},{16,0},{4,20},{20,4},{8,24},{24,8},{12,28},{28,12},{32,48},... | collective-permute-start | bytes 49160 | tf_op jit(solution)/shard_map/ppermute | solution.py:17
  139.3 8.7 %collective-permute-start.10 = (bf16[128,128]{0,1:T(8,128)(2,1)S(1)}, bf16[128,128]{0,1:T(8,128)(2,1)S(1)}, u32[]{:S(2)}, u32[]{:S(2)}) collective-permute-start(bf16[128,128]{0,1:T(8,128)(2,1)S(1)} %maximum_select_fusion.10), channel_id=1, source_target_pairs={{0,32},{32,0},{4,36},{36,4},{8,40},{40,8},{12,44},{44,12},{16,48},... | collective-permute-start | bytes 98312 | tf_op jit(solution)/shard_map/ppermute | solution.py:17
  153.0 8.0 %collective-permute-start.12 = (bf16[128,512]{0,1:T(8,128)(2,1)S(1)}, bf16[128,512]{0,1:T(8,128)(2,1)S(1)}, u32[]{:S(2)}, u32[]{:S(2)}) collective-permute-start(bf16[128,512]{0,1:T(8,128)(2,1)S(1)} %maximum_select_fusion.3), channel_id=1, source_target_pairs={{0,128},{128,0},{4,132},{132,4},{8,136},{136,8},{12,140},{140,12},... | collective-permute-start | bytes 393224 | tf_op jit(solution)/shard_map/ppermute | solution.py:17
  161.1 12.3 %collective-permute-start.13 = (bf16[128,1024]{0,1:T(8,128)(2,1)S(1)}, bf16[128,1024]{0,1:T(8,128)(2,1)S(1)}, u32[]{:S(2)}, u32[]{:S(2)}) collective-permute-start(bf16[128,1024]{0,1:T(8,128)(2,1)S(1)} %maximum_select_fusion.1), channel_id=1, source_target_pairs={{0,256},{256,0},{4,260},{260,4},{8,264},{264,8},{12,268},{268,12},... | collective-permute-start | bytes 786440 | tf_op jit(solution)/shard_map/ppermute | solution.py:17
  174.5 12.0 %collective-permute-start.14 = (bf16[128,16]{0,1:T(8,128)(2,1)S(1)}, bf16[128,16]{0,1:T(8,128)(2,1)S(1)}, u32[]{:S(2)}, u32[]{:S(2)}) collective-permute-start(bf16[128,16]{0,1:T(8,128)(2,1)S(1)} %get-tuple-element.21), channel_id=1, source_target_pairs={{0,4},{4,0},{8,12},{12,8},{16,20},{20,16},{24,28},{28,24},{32,36},... | collective-permute-start | bytes 12296 | tf_op jit(solution)/shard_map/ppermute | solution.py:17
  190.9 5.4 %collective-permute-start.16 = (bf16[128,64]{0,1:T(8,128)(2,1)S(1)}, bf16[128,64]{0,1:T(8,128)(2,1)S(1)}, u32[]{:S(2)}, u32[]{:S(2)}) collective-permute-start(bf16[128,64]{0,1:T(8,128)(2,1)S(1)} %maximum_select_fusion.16), channel_id=1, source_target_pairs={{0,16},{16,0},{4,20},{20,4},{8,24},{24,8},{12,28},{28,12},{32,48},... | collective-permute-start | bytes 49160 | tf_op jit(solution)/shard_map/ppermute | solution.py:17
  196.3 8.6 %collective-permute-start.17 = (bf16[128,128]{0,1:T(8,128)(2,1)S(1)}, bf16[128,128]{0,1:T(8,128)(2,1)S(1)}, u32[]{:S(2)}, u32[]{:S(2)}) collective-permute-start(bf16[128,128]{0,1:T(8,128)(2,1)S(1)} %maximum_select_fusion.11), channel_id=1, source_target_pairs={{0,32},{32,0},{4,36},{36,4},{8,40},{40,8},{12,44},{44,12},{16,48},... | collective-permute-start | bytes 98312 | tf_op jit(solution)/shard_map/ppermute | solution.py:17
  209.9 7.7 %collective-permute-start.19 = (bf16[128,512]{0,1:T(8,128)(2,1)S(1)}, bf16[128,512]{0,1:T(8,128)(2,1)S(1)}, u32[]{:S(2)}, u32[]{:S(2)}) collective-permute-start(bf16[128,512]{0,1:T(8,128)(2,1)S(1)} %maximum_select_fusion.4), channel_id=1, source_target_pairs={{0,128},{128,0},{4,132},{132,4},{8,136},{136,8},{12,140},{140,12},... | collective-permute-start | bytes 393224 | tf_op jit(solution)/shard_map/ppermute | solution.py:17
  221.5 8.5 %collective-permute-start.20 = (bf16[128,16]{0,1:T(8,128)(2,1)S(1)}, bf16[128,16]{0,1:T(8,128)(2,1)S(1)}, u32[]{:S(2)}, u32[]{:S(2)}) collective-permute-start(bf16[128,16]{0,1:T(8,128)(2,1)S(1)} %get-tuple-element.58), channel_id=1, source_target_pairs={{0,4},{4,0},{8,12},{12,8},{16,20},{20,16},{24,28},{28,24},{32,36},... | collective-permute-start | bytes 12296 | tf_op jit(solution)/shard_map/ppermute | solution.py:17
  234.4 5.4 %collective-permute-start.22 = (bf16[128,64]{0,1:T(8,128)(2,1)S(1)}, bf16[128,64]{0,1:T(8,128)(2,1)S(1)}, u32[]{:S(2)}, u32[]{:S(2)}) collective-permute-start(bf16[128,64]{0,1:T(8,128)(2,1)S(1)} %maximum_select_fusion.17), channel_id=1, source_target_pairs={{0,16},{16,0},{4,20},{20,4},{8,24},{24,8},{12,28},{28,12},{32,48},... | collective-permute-start | bytes 49160 | tf_op jit(solution)/shard_map/ppermute | solution.py:17
  239.8 8.6 %collective-permute-start.23 = (bf16[128,128]{0,1:T(8,128)(2,1)S(1)}, bf16[128,128]{0,1:T(8,128)(2,1)S(1)}, u32[]{:S(2)}, u32[]{:S(2)}) collective-permute-start(bf16[128,128]{0,1:T(8,128)(2,1)S(1)} %maximum_select_fusion.12), channel_id=1, source_target_pairs={{0,32},{32,0},{4,36},{36,4},{8,40},{40,8},{12,44},{44,12},{16,48},... | collective-permute-start | bytes 98312 | tf_op jit(solution)/shard_map/ppermute | solution.py:17
  256.7 7.6 %collective-permute-start.25 = (bf16[128,16]{0,1:T(8,128)(2,1)S(1)}, bf16[128,16]{0,1:T(8,128)(2,1)S(1)}, u32[]{:S(2)}, u32[]{:S(2)}) collective-permute-start(bf16[128,16]{0,1:T(8,128)(2,1)S(1)} %get-tuple-element.60), channel_id=1, source_target_pairs={{0,4},{4,0},{8,12},{12,8},{16,20},{20,16},{24,28},{28,24},{32,36},... | collective-permute-start | bytes 12296 | tf_op jit(solution)/shard_map/ppermute | solution.py:17
  268.7 7.7 %collective-permute-start.27 = (bf16[128,64]{0,1:T(8,128)(2,1)S(1)}, bf16[128,64]{0,1:T(8,128)(2,1)S(1)}, u32[]{:S(2)}, u32[]{:S(2)}) collective-permute-start(bf16[128,64]{0,1:T(8,128)(2,1)S(1)} %maximum_select_fusion.18), channel_id=1, source_target_pairs={{0,16},{16,0},{4,20},{20,4},{8,24},{24,8},{12,28},{28,12},{32,48},... | collective-permute-start | bytes 49160 | tf_op jit(solution)/shard_map/ppermute | solution.py:17
  276.4 8.7 %collective-permute-start.28 = (bf16[128,128]{0,1:T(8,128)(2,1)S(1)}, bf16[128,128]{0,1:T(8,128)(2,1)S(1)}, u32[]{:S(2)}, u32[]{:S(2)}) collective-permute-start(bf16[128,128]{0,1:T(8,128)(2,1)S(1)} %maximum_select_fusion.13), channel_id=1, source_target_pairs={{0,32},{32,0},{4,36},{36,4},{8,40},{40,8},{12,44},{44,12},{16,48},... | collective-permute-start | bytes 98312 | tf_op jit(solution)/shard_map/ppermute | solution.py:17
  286.9 5.5 %collective-permute-start.29 = (bf16[128,16]{0,1:T(8,128)(2,1)S(1)}, bf16[128,16]{0,1:T(8,128)(2,1)S(1)}, u32[]{:S(2)}, u32[]{:S(2)}) collective-permute-start(bf16[128,16]{0,1:T(8,128)(2,1)S(1)} %get-tuple-element.62), channel_id=1, source_target_pairs={{0,4},{4,0},{8,12},{12,8},{16,20},{20,16},{24,28},{28,24},{32,36},... | collective-permute-start | bytes 12296 | tf_op jit(solution)/shard_map/ppermute | solution.py:17
  296.8 5.5 %collective-permute-start.31 = (bf16[128,64]{0,1:T(8,128)(2,1)S(1)}, bf16[128,64]{0,1:T(8,128)(2,1)S(1)}, u32[]{:S(2)}, u32[]{:S(2)}) collective-permute-start(bf16[128,64]{0,1:T(8,128)(2,1)S(1)} %maximum_select_fusion.19), channel_id=1, source_target_pairs={{0,16},{16,0},{4,20},{20,4},{8,24},{24,8},{12,28},{28,12},{32,48},... | collective-permute-start | bytes 49160 | tf_op jit(solution)/shard_map/ppermute | solution.py:17
  309.4 6.4 %collective-permute-start.33 = (bf16[128,32]{0,1:T(8,128)(2,1)S(1)}, bf16[128,32]{0,1:T(8,128)(2,1)S(1)}, u32[]{:S(2)}, u32[]{:S(2)}) collective-permute-start(bf16[128,32]{0,1:T(8,128)(2,1)S(1)} %maximum_select_fusion.26), channel_id=1, source_target_pairs={{0,8},{8,0},{4,12},{12,4},{16,24},{24,16},{20,28},{28,20},{32,40},... | collective-permute-start | bytes 24584 | tf_op jit(solution)/shard_map/ppermute | solution.py:17
  (23 other events, 529.4 us)
Sparse Core Ops, SparseCore 0:
  90.5 59.9 all-gather.2
where the time goes:
time: 335 us; the launch traced here: 333 us
  starting transfers between devices  153 us (46%)
  waiting for transfers between devices  125 us (37%)
  matrix products  17.9 us (5%)
  local copies, waits for them, and re-layouts  17 us (5%)
  between operations  15.6 us (5%)
  other arithmetic  4.56 us (1%)
    ppermute x35, starting transfers between devices, partner(): return lax.ppermute(block, axis, route)  153 us
    ppermute x35, waiting for transfers between devices, partner(): return lax.ppermute(block, axis, route)  125 us
    dot_general x6, matrix products, body(): jnp.dot(ancestors, block, preferred_element_type=jnp.float32)  11 us
    another operation x6, local copies, waits for them, and re-layouts, body(): separator_constraint_coupling[0, coff:coff + start * SEP_DEV]  8.19 us
    slice x6, local copies, waits for them, and re-layouts, body(): separator_constraint_coupling[0, coff:coff + start * SEP_DEV]  7.84 us
  transfers between devices with their start and end apart: 36, of which 33 were waited for; matrix products, arithmetic and copies ran while one was open for 10% of the time, Pallas kernels for 0%

commit v1 on v0

v1 whole, which is shorter than its diff:
```python
import jax
import jax.numpy as jnp
from jax import lax
from jax.experimental import pallas as pl
from jax.experimental.pallas import tpu as pltpu
from jax.sharding import PartitionSpec as P

MESH = pl.DeviceIdType.MESH
F32 = jnp.float32
BF16 = jnp.bfloat16
NY, NZ, NC, NX = 8, 8, 2, 4
COLS = 128
LEAF = 640
GROUPS = ((8, 8), (4, 8), (2, 8), (1, 8), (1, 4), (1, 2), (1, 1))
LEVELS = len(GROUPS)
OFF = (0, 2048, 3072, 3584, 3840, 3968, 4032)
CROW = (0, 0, 256, 640, 1088, 1568, 2064)
CHUNKS = (0, 2, 3, 4, 4, 4, 4)
NEAR = 3072
CROWS = 2568


def dot_t(a, b):
    return lax.dot_general(a, b, (((0,), (0,)), ((), ())), preferred_element_type=F32)


def dot(a, b):
    return jnp.dot(a, b, preferred_element_type=F32)


def kernel(
    q_ref, phi_ref, c_hbm, lq_ref, lphi_ref, cpl_hbm, rows_ref,
    sv_ref, out_ref,
    c_flat, c_rows, spread, select, xt, cpl, cps, tail2, tail3,
    ms, mr, qs, qr, bs, br0, br1, br2, m3, m456,
    cl3, cl4, cl5, cl6, pp3, pp4, pp5, pp6,
    k0, k1, k2, k3, k4, k5, k6, pv, acc, kxm, kxe, ps, pr,
    sems,
):
    known = (k0, k1, k2)
    sub = lax.axis_index("sub")
    x = lax.axis_index("col")
    y, z, c = sub // 16, (sub // 2) % 8, sub % 2
    other = 1 - c
    zc = z * 2 + c
    zq = (z % 4) * 2 + c

    counter = [0]

    def new_sems(n):
        first = counter[0]
        counter[0] += n
        return [sems.at[first + i] for i in range(n)]

    def dev(y_, z_, c_):
        return ((y_ * 8 + z_) * 2 + c_, x)

    def send(src, dst, ss, rs, target):
        pltpu.make_async_remote_copy(
            src_ref=src, dst_ref=dst, send_sem=ss, recv_sem=rs,
            device_id=target, device_id_type=MESH,
        ).start()

    def drain(like, sem):
        pltpu.make_async_copy(like, like, sem).wait()

    drains = []

    (c_sem, cpl_sem) = new_sems(2)
    c_copy = pltpu.make_async_copy(c_hbm, c_flat, c_sem)
    c_copy.start()
    cpl_copy = pltpu.make_async_copy(cpl_hbm, cpl, cpl_sem)
    cpl_copy.start()

    barrier = pltpu.get_barrier_semaphore()
    for k in range(1, 16):
        d = (zc + k) % 16
        pl.semaphore_signal(barrier, inc=1, device_id=dev(y, d // 2, d % 2), device_id_type=MESH)
    half, pair = (y // 4) * 4, (y // 2) * 2
    mate = 2 * pair + 1 - y
    for k in range(1, 4):
        for i in range(NZ):
            pl.semaphore_signal(barrier, inc=1, device_id=dev(half + (y + k) % 4, i, c), device_id_type=MESH)
    for i in range(NZ):
        pl.semaphore_signal(barrier, inc=1, device_id=dev(mate, i, other), device_id_type=MESH)
    for k in range(4):
        pl.semaphore_signal(barrier, inc=1, device_id=dev(4 - half + k, z, c), device_id_type=MESH)
    for k in range(1, NX):
        pl.semaphore_signal(barrier, inc=1, device_id=(sub, (x + k) % NX), device_id_type=MESH)

    phi = phi_ref[...].astype(F32)
    qf = q_ref[...].astype(F32)
    lane = lax.broadcasted_iota(jnp.int32, (8, 128), 1)
    for d in range(16):
        h, p = divmod(d, 8)
        parts = [qf[0:32]]
        for g in range(2):
            piece = jnp.zeros((8, 128), F32)
            for b in range(8 * g, min(8 * g + 8, 15)):
                block = phi[:, b * 256 + h * 128 : b * 256 + h * 128 + 128]
                shift = ((b % 8 - p) * 16) % 128
                if shift:
                    block = pltpu.roll(block, shift, 1)
                piece = jnp.where(lax.shift_right_logical(lane, 4) == b % 8, block, piece)
            parts.append(piece)
        ms[d] = jnp.concatenate(parts, axis=0).astype(BF16)
    qs[...] = jnp.concatenate(
        [
            qf[32:56],
            phi[:, 3840:3968],
            jnp.concatenate([phi[:, 3968:4064], jnp.zeros((8, 32), F32)], axis=1),
            jnp.zeros((8, 128), F32),
        ],
        axis=0,
    ).astype(BF16)
    mr[zc] = ms[zc]
    qr[zq] = qs[...]
    pr[x] = jnp.zeros((COLS, LEAF), BF16)

    pl.semaphore_wait(barrier, 15 + 24 + 8 + 4 + NX - 1)

    (a_send, a_recv, q_send, q_recv) = new_sems(4)
    for k in range(1, 16):
        d = (zc + k) % 16
        send(ms.at[d], mr.at[zc], a_send, a_recv, dev(y, d // 2, d % 2))
    for k in range(1, 8):
        d = (zq + k) % 8
        send(qs, qr.at[zq], q_send, q_recv, dev(y, (z // 4) * 4 + d // 2, d % 2))
    drains.append(lambda: drain(mr.at[pl.ds(0, 15)], a_send))
    drains.append(lambda: drain(qr.at[pl.ds(0, 7)], q_send))

    (t_send, f_send, t2_recv, ta_recv, tb_recv) = new_sems(5)
    tail_a, tail_b = tail3.at[pl.ds(0, 512)], tail3.at[pl.ds(512, 512)]
    cpl_copy.wait()

    @pl.when(x == 2)
    def _():
        tail2[0:480] = cpl[528:1008]
        tail2[480:512] = jnp.concatenate([cpl[1008:1016], jnp.zeros((24, LEAF), BF16)], axis=0)
        send(tail2, tail2, t_send, t2_recv, (sub, 1))
        send(tail2, tail2, t_send, t2_recv, (sub, 3))

    @pl.when(x == 3)
    def _():
        tail3[0:992] = cpl[24:1016]
        tail3[992:1024] = jnp.concatenate([jnp.zeros((8, LEAF), BF16), cpl[0:24]], axis=0)
        send(tail_a, tail_a, t_send, ta_recv, (sub, 0))
        send(tail_b, tail_b, t_send, tb_recv, (sub, 2))
        send(tail_b, tail_b, t_send, tb_recv, (sub, 0))
        send(tail_a, tail_a, t_send, ta_recv, (sub, 2))

    def pass_on():
        @pl.when(x == 0)
        def _():
            drain(tail_a, ta_recv)
            send(tail_a, tail_a, f_send, ta_recv, (sub, 1))

        @pl.when(x == 1)
        def _():
            drain(tail2, t2_recv)
            send(tail2, tail2, f_send, t2_recv, (sub, 0))

        @pl.when(x == 2)
        def _():
            drain(tail_b, tb_recv)
            send(tail_b, tail_b, f_send, tb_recv, (sub, 1))

    def finish_tail():
        @pl.when(x == 2)
        def _():
            drain(tail2, t_send)
            drain(tail2, t_send)

        @pl.when(x == 3)
        def _():
            drain(tail3, t_send)
            drain(tail3, t_send)

        @pl.when(x < 3)
        def _():
            drain(tail2, f_send)

    drains.append(finish_tail)

    c_copy.wait()
    wide_row = lax.broadcasted_iota(jnp.int32, (128, 1024), 0)
    wide_col = lax.broadcasted_iota(jnp.int32, (128, 1024), 1)
    spread[...] = jnp.where(lax.shift_right_logical(wide_col, 3) == wide_row, 1.0, 0.0).astype(BF16)
    select[...] = jnp.where((wide_col & 7) == lax.shift_right_logical(wide_row, 4), 1.0, 0.0)

    def rows_of(s):
        steps, each = ((0, 0), (4, 8), (6, 8), (8, 8), (8, 8), (8, 8), (7, 9))[s]

        def step(i, carry):
            for k in range(each):
                row = pl.multiple_of(CROW[s] + (i * each + k) * 8, 8)
                at = pl.multiple_of(row * 128, 1024)
                value = c_flat[0:1, pl.ds(at, 1024)].astype(F32).reshape(8, 128)
                c_rows[pl.ds(row, 8), :] = value
            return carry

        lax.fori_loop(0, steps, step, 0)
        if s == LEVELS - 1:
            c_rows[CROWS : CROWS + 8, :] = jnp.zeros((8, 128), F32)

    def expand(s):
        rows_of(s)

        def step(i, carry):
            rows = c_rows[pl.ds(pl.multiple_of(CROW[s] + i * 128, 8), 128), :].astype(BF16)
            wide = dot_t(rows, spread[...]) * select[...]
            xt[s - 1, :, pl.ds(pl.multiple_of(i * 1024, 1024), 1024)] = wide.astype(BF16)
            return carry

        lax.fori_loop(0, CHUNKS[s], step, 0)

    expand(1)
    expand(2)

    drain(mr.at[pl.ds(0, 15)], a_recv)
    got = mr[...].astype(F32)
    coords = [got[:, 8 * s : 8 * s + 8].reshape(128, 128).astype(BF16) for s in range(4)]
    shapes_lo = got[:, 32:40].reshape(128, 128).astype(BF16)
    shapes_hi = got[:, 40:48].reshape(128, 128).astype(BF16)
    bs[0:8] = dot_t(shapes_lo, coords[0]).reshape(8, 16, 128)
    (b0_send, b0_recv, b1_send, b1_recv, b2_send, b2_recv) = new_sems(6)
    br0[y] = bs[y]
    for k in range(1, NY):
        d = (y + k) % NY
        send(bs.at[d], br0.at[y], b0_send, b0_recv, dev(d, z, c))
    drains.append(lambda: drain(br0.at[pl.ds(0, 7)], b0_send))
    bs[8:12] = dot_t(shapes_hi, coords[1])[0:64].reshape(4, 16, 128)
    br1[y % 4] = bs[8 + y % 4]
    for k in range(1, 4):
        d = (y % 4 + k) % 4
        send(bs.at[8 + d], br1.at[y % 4], b1_send, b1_recv, dev((y // 4) * 4 + d, z, c))
    drains.append(lambda: drain(br1.at[pl.ds(0, 3)], b1_send))
    bs[12:14] = dot_t(shapes_hi, coords[2])[64:96].reshape(2, 16, 128)
    br2[y % 2] = bs[12 + y % 2]
    d = 1 - y % 2
    send(bs.at[12 + d], br2.at[y % 2], b2_send, b2_recv, dev((y // 2) * 2 + d, z, c))
    drains.append(lambda: drain(br2.at[0], b2_send))
    m3[...] = dot_t(shapes_hi, coords[3])[96:112]

    expand(3)

    def publish(s, modal, product):
        if product is not None:
            modal = modal + jnp.sum(product.reshape(8, 16, 128), axis=0)
        value = modal.astype(BF16)
        ny, nz = GROUPS[s]
        known[s][y % ny, z % nz, c] = value
        sv_ref[16 * s : 16 * s + 16, :] = value

    def block_rows(s):
        ny, nz = GROUPS[s]
        return known[s][...].reshape(ny * nz * 32, 128)

    def critical(s):
        width = OFF[s] - OFF[s - 1]
        product = dot(xt[s - 1, :, OFF[s - 1] : OFF[s - 1] + width], block_rows(s - 1))
        if s >= 2:
            product = product + pv[s - 2]
        return product

    def ahead(r):
        count = LEVELS - 2 - r
        width = OFF[r + 1] - OFF[r]
        lhs = xt[r + 1 : LEVELS - 1, :, OFF[r] : OFF[r] + width].reshape(count * 128, width)
        value = dot(lhs, block_rows(r)).reshape(count, 128, 128)
        if r == 0:
            pv[...] = value
        else:
            pv[r:] = pv[r:] + value

    def spread_wide(s, during_first, during_second):
        ny, nz = GROUPS[s]
        k_ref = known[s]
        yi, zi = y % ny, z % nz
        y0, z0 = y - yi, z - zi
        (s1, r1, s2, s3, r3) = new_sems(5)
        r2 = new_sems(max(ny, nz) - 1)

        @pl.when(c == 0)
        def _():
            for k in range(1, ny):
                own = k_ref.at[yi, zi, 0]
                send(own, own, s1, r1, dev(y0 + (yi + k) % ny, z, 0))

        @pl.when(c == 1)
        def _():
            for k in range(1, nz):
                own = k_ref.at[yi, zi, 1]
                send(own, own, s1, r1, dev(y, z0 + (zi + k) % nz, 1))

        during_first()

        @pl.when(c == 0)
        def _():
            drain(k_ref.at[pl.ds(0, ny - 1), 0, 0], r1)
            own = k_ref.at[:, zi, 0]
            for k in range(1, nz):
                send(own, own, s2, r2[k - 1], dev(y, z0 + (zi + k) % nz, 0))
            send(own, own, s3, r3, dev(y, z, 1))

        @pl.when(c == 1)
        def _():
            drain(k_ref.at[0, pl.ds(0, nz - 1), 0], r1)
            own = k_ref.at[yi, :, 1]
            for k in range(1, ny):
                send(own, own, s2, r2[k - 1], dev(y0 + (yi + k) % ny, z, 1))
            send(own, own, s3, r3, dev(y, z, 0))

        during_second()

        def nearest(n):
            return sorted(range(1, n), key=lambda k: (min(k, n - k), k))

        @pl.when(c == 0)
        def _():
            for k in nearest(nz):
                piece = k_ref.at[:, (zi + nz - k) % nz, 0]
                drain(piece, r2[k - 1])
                send(piece, piece, s3, r3, dev(y, z, 1))

        @pl.when(c == 1)
        def _():
            for k in nearest(ny):
                piece = k_ref.at[(yi + ny - k) % ny, :, 1]
                drain(piece, r2[k - 1])
                send(piece, piece, s3, r3, dev(y, z, 0))

        drain(k_ref.at[:, :, 0], r3)

        def finish():
            @pl.when(c == 0)
            def _():
                drain(k_ref.at[pl.ds(0, ny - 1), 0, 0], s1)
                drain(k_ref.at[:, pl.ds(0, nz - 1), 0], s2)

            @pl.when(c == 1)
            def _():
                drain(k_ref.at[0, pl.ds(0, nz - 1), 0], s1)
                drain(k_ref.at[pl.ds(0, ny - 1), :, 0], s2)

            drain(k_ref.at[:, :, 0], s3)

        drains.append(finish)

    def spread_half(during):
        yi = y % 4
        (s0, s1, s3, r3) = new_sems(4)
        r1 = new_sems(4)
        own = k1.at[yi, z, c]
        for k in range(4):
            for i in range(1 if k == 0 else 0, NZ):
                send(own, own, s1 if k else s0, r1[k], dev(half + (y + k) % 4, (z + i) % NZ, c))
        during()
        drain(k1.at[0, pl.ds(0, 7), 0], r1[0])
        for k in (0, 1, 3, 2):
            piece = k1.at[(yi + 4 - k) % 4, :, c]
            if k:
                drain(piece, r1[k])
            send(piece, piece, s3, r3, dev(y, z, other))
        drain(k1.at[:, :, 0], r3)

        def finish():
            drain(k1.at[0, pl.ds(0, 7), 0], s0)
            drain(k1.at[pl.ds(0, 3), :, 0], s1)
            drain(k1.at[:, :, 0], s3)

        drains.append(finish)

    def spread_pair(during):
        (s0, s1, r0, r1) = new_sems(4)
        own = k2.at[y % 2, z, c]
        for k in range(16):
            d = (zc + k) % 16
            send(own, own, s1, r1, dev(mate, d // 2, d % 2))
            if k:
                send(own, own, s0, r0, dev(y, d // 2, d % 2))
        during()
        drain(k0.at[pl.ds(0, 5), pl.ds(0, 3), 0], r0)
        drain(k0.at[pl.ds(0, 4), pl.ds(0, 4), 0], r1)

        def finish():
            drain(k0.at[pl.ds(0, 5), pl.ds(0, 3), 0], s0)
            drain(k0.at[pl.ds(0, 4), pl.ds(0, 4), 0], s1)

        drains.append(finish)

    (xm, xe, p_recv) = new_sems(3)

    def x_send(src, dst, rs, d):
        (ss,) = new_sems(1)

        @pl.when(x != d)
        def _():
            send(src, dst, ss, rs, (sub, d))

        def finish():
            @pl.when(x != d)
            def _():
                drain(src, ss)

        drains.append(finish)

    def stage():
        zeros = jnp.zeros((16, LEAF), BF16)

        @pl.when(x == 0)
        def _():
            cps[0:1008] = cpl[0:1008]
            cps[1008:1024] = jnp.concatenate([cpl[1008:1016], zeros[0:8]], axis=0)

        @pl.when(x == 1)
        def _():
            cps[0:1008] = cpl[8:1016]
            cps[1008:1024] = zeros
            cps[1024:1040] = jnp.concatenate([zeros[0:8], cpl[0:8]], axis=0)

        @pl.when(x == 2)
        def _():
            cps[0:512] = cpl[16:528]
            cps[1024:1040] = cpl[0:16]

        acc[...] = dot(lq_ref[...], lphi_ref[...])

    def partial(xs):
        sends = new_sems(4)

        @pl.when(x == xs)
        def _():
            if xs < 2:
                drain(kxm.at[pl.ds(0, 3)], xm)
            else:
                drain(kxm.at[pl.ds(0, 3), pl.ds(0, 2)], xm)
            if xs:
                drain(kxe.at[pl.ds(0, 3)], xe)
            for p in range(NX):
                mine = p == xs
                if xs == 0:
                    main = (k0[0:4] if mine else kxm[p]).reshape(1024, 128)
                    extra = None
                elif xs == 1:
                    main = (k0[4:8] if mine else kxm[p]).reshape(1024, 128)
                    extra = k0[3, 7, 1] if mine else kxe[p]
                else:
                    main = (k1[0:2] if mine else kxm[p, 0:2]).reshape(512, 128)
                    extra = k0[7, 7, 1] if mine else kxe[p]
                value = dot_t(main, cps[0 : main.shape[0]])
                if extra is not None:
                    value = value + dot_t(extra, cps[1024 : 1024 + extra.shape[0]])
                if mine:
                    acc[...] += value
                else:
                    ps[p] = value.astype(BF16)
                    send(ps.at[p], pr.at[xs], sends[p], p_recv, (sub, p))

        def finish():
            @pl.when(x == xs)
            def _():
                for p in range(NX):
                    if p != xs:
                        drain(ps.at[p], sends[p])

        drains.append(finish)

    drain(br0.at[pl.ds(0, 7)], b0_recv)
    publish(0, jnp.sum(br0[...], axis=0), None)

    def second_0():
        pass_on()
        expand(5)

    spread_wide(0, lambda: expand(4), second_0)

    drain(br1.at[pl.ds(0, 3)], b1_recv)
    publish(1, jnp.sum(br1[...], axis=0), critical(1))

    (c3_send, c3_recv, c4_send, c4_recv, c5_send, c5_recv, c6_send, c6_recv) = new_sems(8)
    (p3_send, p3_recv, p4_send, p4_recv, p5_send, p5_recv, p6_send, p6_recv) = new_sems(8)
    near4, near5, near6 = zq, zq % 4, c

    def to_near(b3, b4, b5, b6, sems_):
        s3, r3, s4, r4, s5, r5, s6, r6 = sems_
        for k in range(1, 16):
            d = (zc + k) % 16
            send(b3.at[zc], b3.at[zc], s3, r3, dev(y, d // 2, d % 2))
        for k in range(1, 8):
            d = (near4 + k) % 8
            send(b4.at[near4], b4.at[near4], s4, r4, dev(y, (z // 4) * 4 + d // 2, d % 2))
        for k in range(1, 4):
            d = (near5 + k) % 4
            send(b5.at[near5], b5.at[near5], s5, r5, dev(y, (z // 2) * 2 + d // 2, d % 2))
        send(b6.at[near6], b6.at[near6], s6, r6, dev(y, z, other))

        def finish():
            drain(b3.at[pl.ds(0, 15)], s3)
            drain(b4.at[pl.ds(0, 7)], s4)
            drain(b5.at[pl.ds(0, 3)], s5)
            drain(b6.at[0], s6)

        drains.append(finish)

    def during_1():
        x_send(k0.at[pl.ds(0, 4)], kxm.at[x], xm, 0)
        x_send(k0.at[pl.ds(4, 4)], kxm.at[x], xm, 1)
        x_send(k0.at[3, 7, 1], kxe.at[x], xe, 1)
        x_send(k0.at[7, 7, 1], kxe.at[x], xe, 2)
        expand(6)
        ahead(0)

        def fold(s, width):
            wide = xt[s - 1, :, NEAR : NEAR + width].astype(F32)
            return jnp.sum(wide.reshape(8, 16, width), axis=0).astype(BF16)

        cl3[zc] = fold(3, 512)
        cl4[near4] = fold(4, 768)
        cl5[near5] = fold(5, 896)
        cl6[near6] = fold(6, 1024)
        to_near(cl3, cl4, cl5, cl6, (c3_send, c3_recv, c4_send, c4_recv, c5_send, c5_recv, c6_send, c6_recv))

        drain(qr.at[pl.ds(0, 7)], q_recv)
        near = qr[...].astype(F32)
        member = lax.shift_right_logical(lax.broadcasted_iota(jnp.int32, (64, 128), 0), 3)
        q4, q5, q6 = [near[:, 8 * i : 8 * i + 8].reshape(64, 128) for i in range(3)]
        q5 = jnp.where(lax.shift_right_logical(member, 2) == (z % 4) // 2, q5, 0.0)
        q6 = jnp.where(lax.shift_right_logical(member, 1) == z % 4, q6, 0.0)
        hi = near[:, 24:32].reshape(64, 128).astype(BF16)
        lo = near[:, 32:40].reshape(64, 128).astype(BF16)
        m456[0] = dot_t(hi, q4.astype(BF16))
        m456[1] = dot_t(lo, q5.astype(BF16))
        m456[2] = dot_t(lo, q6.astype(BF16))

    spread_half(during_1)

    drain(br2.at[0], b2_recv)
    publish(2, jnp.sum(br2[...], axis=0), critical(2))

    def during_2():
        ahead(1)

        def prefix(s, modal):
            return (modal + jnp.sum(pv[s - 2].reshape(8, 16, 128), axis=0)).astype(BF16)

        def own_rows(s, at):
            return m456[s - 4, pl.ds(pl.multiple_of(at, 16), 16), :]

        pp3[zc] = prefix(3, m3[...])
        pp4[near4] = prefix(4, own_rows(4, near4 * 16))
        pp5[near5] = prefix(5, own_rows(5, near5 * 16))
        pp6[near6] = prefix(6, own_rows(6, 64 + near6 * 16))
        to_near(pp3, pp4, pp5, pp6, (p3_send, p3_recv, p4_send, p4_recv, p5_send, p5_recv, p6_send, p6_recv))
        x_send(k1.at[pl.ds(0, 2)], kxm.at[x, pl.ds(0, 2)], xm, 2)
        stage()
        partial(0)
        partial(1)

        @pl.when((x == 0) | (x == 3))
        def _():
            drain(tail2, t2_recv)

        acc[...] += dot_t(k1[2:4].reshape(512, 128), tail2[...])
        partial(2)

    spread_pair(during_2)

    drain(cl3.at[pl.ds(0, 15)], c3_recv)
    drain(cl4.at[pl.ds(0, 7)], c4_recv)
    drain(cl5.at[pl.ds(0, 3)], c5_recv)
    drain(cl6.at[0], c6_recv)
    drain(pp3.at[pl.ds(0, 15)], p3_recv)
    drain(pp4.at[pl.ds(0, 7)], p4_recv)
    drain(pp5.at[pl.ds(0, 3)], p5_recv)
    drain(pp6.at[0], p6_recv)
    above2 = block_rows(2)
    c3, c4 = cl3[...].reshape(256, 512), cl4[...].reshape(128, 768)
    c5, c6 = cl5[...].reshape(64, 896), cl6[...].reshape(32, 1024)
    first = dot(jnp.concatenate([c3, c4[:, 0:512], c5[:, 0:512], c6[:, 0:512]], axis=0), above2)
    above3 = (pp3[...].reshape(256, 128).astype(F32) + first[0:256]).astype(BF16)
    second = dot(jnp.concatenate([c4[:, 512:768], c5[:, 512:768], c6[:, 512:768]], axis=0), above3) + first[256:480]
    above4 = (pp4[...].reshape(128, 128).astype(F32) + second[0:128]).astype(BF16)
    third = dot(jnp.concatenate([c5[:, 768:896], c6[:, 768:896]], axis=0), above4) + second[128:224]
    above5 = (pp5[...].reshape(64, 128).astype(F32) + third[0:64]).astype(BF16)
    above6 = pp6[...].reshape(32, 128).astype(F32) + third[64:96] + dot(c6[:, 896:960], above5)
    above6 = above6.astype(BF16)
    k3[...] = above3.reshape(16, 16, 128)
    k4[...] = above4.reshape(8, 16, 128)
    k5[...] = above5.reshape(4, 16, 128)
    k6[...] = above6.reshape(2, 16, 128)
    sv_ref[48:64, :] = k3[zc]
    sv_ref[64:80, :] = k4[near4]
    sv_ref[80:96, :] = k5[near5]
    sv_ref[96:112, :] = k6[near6]

    @pl.when(x < 2)
    def _():
        drain(tail_b, tb_recv)

    @pl.when((x == 1) | (x == 2))
    def _():
        drain(tail_a, ta_recv)

    late = jnp.concatenate([above2, above3, above4, above5, above6, k1[3, 7].reshape(32, 128)], axis=0)
    total = acc[...] + dot_t(late, tail3[...])

    @pl.when(x == 3)
    def _():
        drain(pr.at[pl.ds(0, 3)], p_recv)

    @pl.when(x < 3)
    def _():
        drain(pr.at[pl.ds(0, 2)], p_recv)

    for p in range(NX - 1):
        total = total + pr[p].astype(F32)
    live = lax.broadcasted_iota(jnp.int32, (COLS, LEAF), 1) < rows_ref[0]
    out_ref[...] = jnp.where(live, total, 0.0).astype(BF16)
    for finish in drains:
        finish()


def hand_over(values, leaf, values_out, leaf_out):
    leaf_out[...] = leaf[...]
    values_out[...] = values[...]


N_SEMS = 112


def body(sep_q, sep_phi, coupling, leaf_q, leaf_phi, leaf_coupling, leaf_rows):
    vmem = pl.BlockSpec(memory_space=pltpu.VMEM)
    hbm = pl.BlockSpec(memory_space=pl.ANY)
    block = (16, 128)
    scratch = [
        pltpu.VMEM((1, 328704), BF16),
        pltpu.VMEM((CROWS + 8, 128), F32),
        pltpu.VMEM((128, 1024), BF16),
        pltpu.VMEM((128, 1024), F32),
        pltpu.VMEM((LEVELS - 1, 128, 4096), BF16),
        pltpu.VMEM((1016, LEAF), BF16),
        pltpu.VMEM((1040, LEAF), BF16),
        pltpu.VMEM((512, LEAF), BF16),
        pltpu.VMEM((1024, LEAF), BF16),
        pltpu.VMEM((16, 48, 128), BF16),
        pltpu.VMEM((16, 48, 128), BF16),
        pltpu.VMEM((48, 128), BF16),
        pltpu.VMEM((8, 48, 128), BF16),
        pltpu.VMEM((14,) + block, F32),
        pltpu.VMEM((8,) + block, F32),
        pltpu.VMEM((4,) + block, F32),
        pltpu.VMEM((2,) + block, F32),
        pltpu.VMEM(block, F32),
        pltpu.VMEM((3, 128, 128), F32),
        pltpu.VMEM((16, 16, 512), BF16),
        pltpu.VMEM((8, 16, 768), BF16),
        pltpu.VMEM((4, 16, 896), BF16),
        pltpu.VMEM((2, 16, 1024), BF16),
    ]
    scratch += [pltpu.VMEM((n,) + block, BF16) for n in (16, 8, 4, 2)]
    scratch += [pltpu.VMEM(group + (NC,) + block, BF16) for group in GROUPS[:3]]
    scratch += [pltpu.VMEM((n,) + block, BF16) for n in (16, 8, 4, 2)]
    scratch += [
        pltpu.VMEM((LEVELS - 2, 128, 128), F32),
        pltpu.VMEM((COLS, LEAF), F32),
        pltpu.VMEM((NX, 4, NZ, NC) + block, BF16),
        pltpu.VMEM((NX,) + block, BF16),
        pltpu.VMEM((NX, COLS, LEAF), BF16),
        pltpu.VMEM((NX, COLS, LEAF), BF16),
        pltpu.SemaphoreType.DMA((N_SEMS,)),
    ]
    values, leaf = pl.pallas_call(
        kernel,
        out_shape=(
            jax.ShapeDtypeStruct((16 * LEVELS, COLS), BF16),
            jax.ShapeDtypeStruct((COLS, LEAF), BF16),
        ),
        in_specs=[vmem, vmem, hbm, vmem, vmem, hbm, pl.BlockSpec(memory_space=pltpu.SMEM)],
        out_specs=(vmem, vmem),
        scratch_shapes=scratch,
        compiler_params=pltpu.CompilerParams(
            collective_id=0, has_side_effects=True, vmem_limit_bytes=56 * 1024 * 1024
        ),
        cost_estimate=pl.CostEstimate(flops=2_000_000_000, bytes_accessed=4_000_000, transcendentals=0),
    )(sep_q[0].T, sep_phi[0], coupling, leaf_q[0], leaf_phi[0], leaf_coupling[0], leaf_rows)
    values, leaf = pl.pallas_call(
        hand_over,
        out_shape=(
            jax.ShapeDtypeStruct((16 * LEVELS, COLS), BF16),
            jax.ShapeDtypeStruct((COLS, LEAF), BF16),
        ),
        in_specs=[vmem, vmem],
        out_specs=(vmem, vmem),
        compiler_params=pltpu.CompilerParams(vmem_limit_bytes=56 * 1024 * 1024),
    )(values, leaf)
    return values.T[None], leaf[None]


def solution(mesh):
    in_specs = (
        P("sub", "col", None),
        P("sub", None, None),
        P("sub", None),
        P("sub", "col", None),
        P("sub", None, None),
        P("sub", "col", None),
        P("sub"),
    )
    out_specs = (P("sub", "col", None), P("sub", "col", None))
    return jax.shard_map(body, mesh=mesh, in_specs=in_specs, out_specs=out_specs, check_vma=False)
```

time: 335 us -> 73.9 us (0.22)
  the two profiles are of different devices: /device:TPU:1 before, /device:TPU:14 now
where the time goes in v1:
time: 73.9 us; the launch traced here: 73.8 us
  Pallas kernels  72.5 us (98%)
  between operations  1.29 us (2%)
    pallas_call x1, Pallas kernels, body(): pl.pallas_call(kernel, out_shape=(jax.ShapeDtypeStruct((16 * LEVELS, COLS...  70.9 us
    pallas_call x1, Pallas kernels, body(): pl.pallas_call(hand_over, out_shape=(jax.ShapeDtypeStruct((16 * LEVELS, C...  1.62 us

profile of v1, /device:TPU:14, one launch (start us, length us, event | category | flops | bytes accessed | tf_op | source)
XLA Modules:
  0.0 73.8 jit_solution(14407422165568333041)
XLA Ops:
  1.3 70.9 %shard_map.86 = (bf16[112,128]{1,0:T(8,128)(2,1)}, bf16[128,640]{1,0:T(8,128)(2,1)}) custom-call(bf16[56,128]{1,0:T(8,128)(2,1)} %bitcast.17, bf16[8,4064]{1,0:T(8,128)(2,1)} %bitcast.14, bf16[1,328704]{1,0:T(2,128)(2,1)} %c_hbm.1, bf16[128,128]{1,0:T(8,128)(2,1)} %bitcast.15, bf16[128,640]{1,0:T(8,128)(2,1)} %bitcast.12, bf16[1016,640]{1,0:T(8,128)(2,1)} %bitcast.11, ...), custom_call_target="tpu_custom_call" | custom-call | flops 2000000000 | bytes 4000000 | tf_op jit(solution)/shard_map/pallas_call | solution.py:673
  72.1 1.6 %shard_map.87 = (bf16[112,128]{1,0:T(8,128)(2,1)}, bf16[128,640]{1,0:T(8,128)(2,1)}) custom-call(bf16[112,128]{1,0:T(8,128)(2,1)} %get-tuple-element.6.values, bf16[128,640]{1,0:T(8,128)(2,1)} %get-tuple-element.7.leaf), custom_call_target="tpu_custom_call" | custom-call | tf_op jit(solution)/shard_map/pallas_call | solution.py:687

commit v2 on v1

v2 whole, which is shorter than its diff:
```python
import jax
import jax.numpy as jnp
from jax import lax
from jax.experimental import pallas as pl
from jax.experimental.pallas import tpu as pltpu
from jax.sharding import PartitionSpec as P

MESH = pl.DeviceIdType.MESH
F32 = jnp.float32
BF16 = jnp.bfloat16
NY, NZ, NC, NX = 8, 8, 2, 4
COLS = 128
LEAF = 640
GROUPS = ((8, 8), (4, 8), (2, 8), (1, 8), (1, 4), (1, 2), (1, 1))
LEVELS = len(GROUPS)
CROW = (0, 0, 256, 640, 1088, 1568, 2064)
NEAR = 3072
CL_AT = (0, 512, 1280, 2176, 3200)
CROWS = 2568


def dot_t(a, b):
    return lax.dot_general(a, b, (((0,), (0,)), ((), ())), preferred_element_type=F32)


def dot(a, b):
    return jnp.dot(a, b, preferred_element_type=F32)


def kernel(
    q_hbm, phi_hbm, c_hbm, lq_hbm, lphi_hbm, cpl_hbm, rows_ref,
    sv_ref, out_ref,
    q_ref, phi_ref, lq_ref, lphi_ref, c_flat, c_rows, spread, select, ct0, ct1, k32, kp0, kp1, cg,
    ms, mr, bs, br0, br1, br2, m3, m456, cl,
    k0, k1, kq, k3, k4, k5, k6, pv, acc,
    sems,
):
    known = (k0, k1)
    sub = lax.axis_index("sub")
    x = lax.axis_index("col")
    y, z, c = sub // 16, (sub // 2) % 8, sub % 2
    other = 1 - c
    zc = z * 2 + c
    zq = (z % 4) * 2 + c

    counter = [0]

    def new_sems(n):
        first = counter[0]
        counter[0] += n
        return [sems.at[first + i] for i in range(n)]

    def dev(y_, z_, c_):
        return ((y_ * 8 + z_) * 2 + c_, x)

    def send(src, dst, ss, rs, target):
        pltpu.make_async_remote_copy(
            src_ref=src, dst_ref=dst, send_sem=ss, recv_sem=rs,
            device_id=target, device_id_type=MESH,
        ).start()

    def drain(like, sem):
        pltpu.make_async_copy(like, like, sem).wait()

    drains = []

    fetches = []
    for src, dst, sem in zip(
        (q_hbm, phi_hbm, c_hbm, cpl_hbm, lq_hbm, lphi_hbm),
        (q_ref, phi_ref, c_flat, cg.at[x], lq_ref, lphi_ref),
        new_sems(6),
    ):
        fetches.append(pltpu.make_async_copy(src, dst, sem))
        fetches[-1].start()
    q_copy, phi_copy, c_copy, cpl_copy, lq_copy, lphi_copy = fetches

    barrier = pltpu.get_barrier_semaphore()
    for k in range(1, 16):
        d = (zc + k) % 16
        pl.semaphore_signal(barrier, inc=1, device_id=dev(y, d // 2, d % 2), device_id_type=MESH)
    half, pair = (y // 4) * 4, (y // 2) * 2
    mate = 2 * pair + 1 - y
    for k in range(1, 4):
        for i in range(NZ):
            pl.semaphore_signal(barrier, inc=1, device_id=dev(half + (y + k) % 4, i, c), device_id_type=MESH)
    for i in range(NZ):
        pl.semaphore_signal(barrier, inc=1, device_id=dev(mate, i, other), device_id_type=MESH)
    for k in range(4):
        pl.semaphore_signal(barrier, inc=1, device_id=dev(4 - half + k, z, c), device_id_type=MESH)
    for k in (1, NX - 1):
        pl.semaphore_signal(barrier, inc=1, device_id=(sub, (x + k) % NX), device_id_type=MESH)

    q_copy.wait()
    phi_copy.wait()
    phi = phi_ref[...].astype(F32)
    qf = q_ref[...].astype(F32)
    lane = lax.broadcasted_iota(jnp.int32, (8, 128), 1)
    zero = jnp.zeros((8, 128), F32)
    shared = [
        qf[32:40],
        phi[:, 3840:3968],
        qf[40:48],
        jnp.concatenate([phi[:, 3968:4064], zero[:, 0:32]], axis=1),
        qf[48:56],
        zero,
    ]
    for d in range(16):
        h, p = divmod(d, 8)
        parts = [qf[0:32]]
        for g in range(2):
            piece = jnp.zeros((8, 128), F32)
            for b in range(8 * g, min(8 * g + 8, 15)):
                block = phi[:, b * 256 + h * 128 : b * 256 + h * 128 + 128]
                shift = ((b % 8 - p) * 16) % 128
                if shift:
                    block = pltpu.roll(block, shift, 1)
                piece = jnp.where(lax.shift_right_logical(lane, 4) == b % 8, block, piece)
            parts.append(piece)
        ms[d] = jnp.concatenate(parts + shared, axis=0).astype(BF16)
    mr[zc] = ms[zc]

    pl.semaphore_wait(barrier, 15 + 24 + 8 + 4 + 2)

    base4, base5, base6 = zc - zq, zc - zc % 4, zc - c
    near4, near5, near6 = zq, zc % 4, c
    classes = (
        [8 - base4 + (near4 + i) % 8 for i in range(8)],
        [base4 + 4 - (base5 - base4) + (near5 + i) % 4 for i in range(4)],
        [base5 + 2 - (base6 - base5) + (near6 + i) % 2 for i in range(2)],
        [base6 + other],
    )

    def to_row(source, like):
        ss, rs = new_sems(4), new_sems(4)
        for n, places in enumerate(classes):
            for d in places:
                src, dst = source(n, d)
                send(src, dst, ss[n], rs[n], dev(y, d // 2, d % 2))

        def wait(sems_):
            for n, places in enumerate(classes):
                drain(like(n, len(places)), sems_[n])

        drains.append(lambda: wait(ss))
        return lambda: wait(rs)

    def factors(n, d):
        return ms.at[d, pl.ds(0, 48 + 16 * n)], mr.at[zc, pl.ds(0, 48 + 16 * n)]

    wait_factors = to_row(factors, lambda n, count: mr.at[pl.ds(0, count), pl.ds(0, 48 + 16 * n)])

    lanes = (pl.ds(0, 384), pl.ds(384, 256))
    left, right = (x + NX - 1) % NX, (x + 1) % NX
    (gr_send, gl_send, fr_send, fl_send, l0, l1, r0, r1, o_l, o_r) = new_sems(10)

    def by_core(step):
        for core in range(NC):
            @pl.when(c == core)
            def _(core=core):
                step(lanes[core], lanes[1 - core])

    def give(one, two):
        for part, rs_right in ((one, l0), (two, l1)):
            send(cpl_hbm.at[:, part], cg.at[x, :, part], gr_send, rs_right, (sub, right))
        for part, rs_left in ((two, r0), (one, r1)):
            send(cpl_hbm.at[:, part], cg.at[x, :, part], gl_send, rs_left, (sub, left))

    def pass_on(one, two):
        piece = cg.at[left, :, one]
        drain(piece, l0)
        send(piece, piece, fr_send, o_l, (sub, right))
        piece = cg.at[right, :, two]
        drain(piece, r0)
        send(piece, piece, fl_send, o_r, (sub, left))

    def wait_neighbours(one, two):
        drain(cg.at[0, :, two], l1)
        drain(cg.at[0, :, one], r1)

    def wait_opposite(one, two):
        drain(cg.at[0, :, one], o_l)
        drain(cg.at[0, :, two], o_r)

    def finish_gather(one, two):
        drain(cg.at[0], gr_send)
        drain(cg.at[0], gl_send)
        drain(cg.at[0, :, one], fr_send)
        drain(cg.at[0, :, two], fl_send)

    by_core(give)
    drains.append(lambda: by_core(finish_gather))

    c_copy.wait()
    wide_row = lax.broadcasted_iota(jnp.int32, (128, 1024), 0)
    wide_col = lax.broadcasted_iota(jnp.int32, (128, 1024), 1)
    spread[...] = jnp.where(lax.shift_right_logical(wide_col, 3) == wide_row, 1.0, 0.0).astype(BF16)
    select[...] = jnp.where((wide_col & 7) == lax.shift_right_logical(wide_row, 4), 1.0, 0.0)

    def rows_of(first, steps, each):
        def step(i, carry):
            for k in range(each):
                row = pl.multiple_of(first + (i * each + k) * 8, 8)
                at = pl.multiple_of(row * 128, 1024)
                value = c_flat[0:1, pl.ds(at, 1024)].astype(F32).reshape(8, 128)
                c_rows[pl.ds(row, 8), :] = value
            return carry

        lax.fori_loop(0, steps, step, 0)

    def arrange(s):
        rows_of(CROW[s], 4 if s == 1 else 6, 8)
        for k in range(2 if s == 1 else 3):
            block = c_rows[CROW[s] + 128 * k : CROW[s] + 128 * k + 128, :].T.astype(BF16)
            for j in range(8):
                piece = block[16 * j : 16 * j + 16]
                if k < 2:
                    ct0[s - 1, :, 256 * j + 128 * k : 256 * j + 128 * k + 128] = piece
                else:
                    ct1[s - 2, :, 128 * j : 128 * j + 128] = piece

    def dense(s, at, width):
        first = CROW[s] + NEAR // 8
        rows_of(first, *((3, 5) if s == LEVELS - 1 else (2, 8)))
        if s == LEVELS - 1:
            c_rows[CROWS : CROWS + 8, :] = jnp.zeros((8, 128), F32)
        wide = dot_t(c_rows[first : first + 128, :].astype(BF16), spread[:, 0:width]) * select[:, 0:width]
        cl[zc, :, at : at + width] = jnp.sum(wide.reshape(8, 16, width), axis=0).astype(BF16)

    for s, (at, end) in enumerate(zip(CL_AT, CL_AT[1:])):
        dense(3 + s, at, end - at)

    wait_factors()
    got = mr[:, 0:48].astype(F32)
    coords = [got[:, 8 * s : 8 * s + 8].reshape(128, 128).astype(BF16) for s in range(4)]
    shapes_lo = got[:, 32:40].reshape(128, 128).astype(BF16)
    shapes_hi = got[:, 40:48].reshape(128, 128).astype(BF16)
    bs[0:8] = dot_t(shapes_lo, coords[0]).reshape(8, 16, 128)
    (b0_send, b0_recv, b1_send, b1_recv, b2_send, b2_recv) = new_sems(6)
    br0[y] = bs[y]
    for k in range(1, NY):
        d = (y + k) % NY
        send(bs.at[d], br0.at[y], b0_send, b0_recv, dev(d, z, c))
    drains.append(lambda: drain(br0.at[pl.ds(0, 7)], b0_send))
    bs[8:12] = dot_t(shapes_hi, coords[1])[0:64].reshape(4, 16, 128)
    br1[y % 4] = bs[8 + y % 4]
    for k in range(1, 4):
        d = (y % 4 + k) % 4
        send(bs.at[8 + d], br1.at[y % 4], b1_send, b1_recv, dev((y // 4) * 4 + d, z, c))
    drains.append(lambda: drain(br1.at[pl.ds(0, 3)], b1_send))
    bs[12:14] = dot_t(shapes_hi, coords[2])[64:96].reshape(2, 16, 128)
    br2[y % 2] = bs[12 + y % 2]
    d = 1 - y % 2
    send(bs.at[12 + d], br2.at[y % 2], b2_send, b2_recv, dev((y // 2) * 2 + d, z, c))
    drains.append(lambda: drain(br2.at[0], b2_send))
    m3[...] = dot_t(shapes_hi, coords[3])[96:112]

    def lookahead(n, d):
        piece = cl.at[zc, :, pl.ds(0, CL_AT[n + 1])]
        return piece, piece

    wait_lookahead = to_row(lookahead, lambda n, count: cl.at[pl.ds(0, count), :, pl.ds(0, CL_AT[n + 1])])

    quad = mr[pl.ds(base4, 8), 48:64].astype(F32)
    two = mr[pl.ds(base5, 4), 64:80].astype(F32)
    chip = mr[pl.ds(base6, 2), 64:96].astype(F32)

    def part(block, at):
        return block[:, at : at + 8].reshape(-1, 128).astype(BF16)

    m456[0] = dot_t(part(quad, 8), part(quad, 0))
    m456[1] = dot_t(part(two, 8), part(two, 0))
    m456[2] = dot_t(part(chip, 8), part(chip, 16))
    arrange(1)

    def publish(s, modal):
        value = modal.astype(BF16)
        ny, nz = GROUPS[s]
        known[s][y % ny, z % nz, c] = value
        sv_ref[16 * s : 16 * s + 16, :] = value

    def permute(k_ref, kp):
        rows = kp.shape[0]
        each = rows // 8
        k32[0:rows] = k_ref[...].reshape(rows, 128).astype(F32)
        for j in range(8):
            kp[each * j : each * j + each] = k32[pl.ds(j, each, stride=8), :].astype(BF16)

    def spread_wide(s, during_first, during_second):
        ny, nz = GROUPS[s]
        k_ref = known[s]
        yi, zi = y % ny, z % nz
        y0, z0 = y - yi, z - zi
        (s1, r1, s2, s3, r3) = new_sems(5)
        r2 = new_sems(max(ny, nz) - 1)

        @pl.when(c == 0)
        def _():
            for k in range(1, ny):
                own = k_ref.at[yi, zi, 0]
                send(own, own, s1, r1, dev(y0 + (yi + k) % ny, z, 0))

        @pl.when(c == 1)
        def _():
            for k in range(1, nz):
                own = k_ref.at[yi, zi, 1]
                send(own, own, s1, r1, dev(y, z0 + (zi + k) % nz, 1))

        during_first()

        @pl.when(c == 0)
        def _():
            drain(k_ref.at[pl.ds(0, ny - 1), 0, 0], r1)
            own = k_ref.at[:, zi, 0]
            for k in range(1, nz):
                send(own, own, s2, r2[k - 1], dev(y, z0 + (zi + k) % nz, 0))
            send(own, own, s3, r3, dev(y, z, 1))

        @pl.when(c == 1)
        def _():
            drain(k_ref.at[0, pl.ds(0, nz - 1), 0], r1)
            own = k_ref.at[yi, :, 1]
            for k in range(1, ny):
                send(own, own, s2, r2[k - 1], dev(y0 + (yi + k) % ny, z, 1))
            send(own, own, s3, r3, dev(y, z, 0))

        during_second()

        def nearest(n):
            return sorted(range(1, n), key=lambda k: (min(k, n - k), k))

        @pl.when(c == 0)
        def _():
            for k in nearest(nz):
                piece = k_ref.at[:, (zi + nz - k) % nz, 0]
                drain(piece, r2[k - 1])
                send(piece, piece, s3, r3, dev(y, z, 1))

        @pl.when(c == 1)
        def _():
            for k in nearest(ny):
                piece = k_ref.at[(yi + ny - k) % ny, :, 1]
                drain(piece, r2[k - 1])
                send(piece, piece, s3, r3, dev(y, z, 0))

        drain(k_ref.at[:, :, 0], r3)

        def finish():
            @pl.when(c == 0)
            def _():
                drain(k_ref.at[pl.ds(0, ny - 1), 0, 0], s1)
                drain(k_ref.at[:, pl.ds(0, nz - 1), 0], s2)

            @pl.when(c == 1)
            def _():
                drain(k_ref.at[0, pl.ds(0, nz - 1), 0], s1)
                drain(k_ref.at[pl.ds(0, ny - 1), :, 0], s2)

            drain(k_ref.at[:, :, 0], s3)

        drains.append(finish)

    def spread_half(during):
        yi = y % 4
        (s0, s1, s3, r3) = new_sems(4)
        r1 = new_sems(4)
        own = k1.at[yi, z, c]
        for k in range(4):
            for i in range(1 if k == 0 else 0, NZ):
                send(own, own, s1 if k else s0, r1[k], dev(half + (y + k) % 4, (z + i) % NZ, c))
        during()
        drain(k1.at[0, pl.ds(0, 7), 0], r1[0])
        for k in (0, 1, 3, 2):
            piece = k1.at[(yi + 4 - k) % 4, :, c]
            if k:
                drain(piece, r1[k])
            send(piece, piece, s3, r3, dev(y, z, other))
        drain(k1.at[:, :, 0], r3)

        def finish():
            drain(k1.at[0, pl.ds(0, 7), 0], s0)
            drain(k1.at[pl.ds(0, 3), :, 0], s1)
            drain(k1.at[:, :, 0], s3)

        drains.append(finish)

    def spread_pair(during):
        yi = y % 2
        (s1, r1) = new_sems(2)
        own = kq.at[yi, zc, 0]

        def with_sums(n, d):
            piece = kq.at[yi, zc, pl.ds(0, 2 + n)]
            return piece, piece

        wait_row = to_row(with_sums, lambda n, count: kq.at[0, pl.ds(0, count), pl.ds(0, 2 + n)])
        for k in range(16):
            d = (zc + k) % 16
            send(own, own, s1, r1, dev(mate, d // 2, d % 2))
        during()
        wait_row()
        drain(kq.at[0, :, 0], r1)
        drains.append(lambda: drain(kq.at[0, :, 0], s1))

    def ancestors(block):
        first = k0[...].reshape(2048, 128)
        if block < 2:
            return first[1016 * block : 1016 * block + 1016]
        return jnp.concatenate([first[2032:], k1[...].reshape(1024, 128)[0:1000]], axis=0)

    drain(br0.at[pl.ds(0, 7)], b0_recv)
    publish(0, jnp.sum(br0[...], axis=0))

    def first_0():
        arrange(2)
        arrange(3)

    def second_0():
        arrange(4)
        arrange(5)
        by_core(pass_on)

    spread_wide(0, first_0, second_0)

    permute(k0, kp0)
    drain(br1.at[pl.ds(0, 3)], b1_recv)
    publish(1, jnp.sum(br1[...], axis=0) + dot(ct0[0], kp0[...]))

    def during_1():
        arrange(6)
        pv[...] = dot(ct0[1:6].reshape(80, 2048), kp0[...]).reshape(5, 16, 128)
        lq_copy.wait()
        lphi_copy.wait()
        acc[...] = dot(lq_ref[...], lphi_ref[...])

    spread_half(during_1)

    permute(k1, kp1)
    drain(br2.at[0], b2_recv)
    product = dot(ct1[...].reshape(80, 1024), kp1[...]) + pv[...].reshape(80, 128)

    def own_rows(s, at):
        return m456[s - 4, pl.ds(pl.multiple_of(at, 16), 16), :]

    blocks = (
        product[0:16] + jnp.sum(br2[...], axis=0),
        product[16:32] + m3[...],
        product[32:48] + own_rows(4, near4 * 16),
        product[48:64] + own_rows(5, near5 * 16),
        product[64:80] + own_rows(6, 64 + near6 * 16),
    )
    for n, value in enumerate(blocks):
        kq[y % 2, zc, n] = value.astype(BF16)
    sv_ref[32:48, :] = blocks[0].astype(BF16)

    def during_2():
        cpl_copy.wait()
        by_core(wait_neighbours)
        for block in range(3):
            @pl.when((block + NX - x) % NX != 2)
            def _(block=block):
                acc[...] += dot_t(ancestors(block), cg[block])

    spread_pair(during_2)

    wait_lookahead()
    above2 = kq[:, :, 0].reshape(512, 128)
    yi = y % 2
    pp3 = kq[yi, :, 1].reshape(256, 128).astype(F32)
    pp4 = kq[yi, pl.ds(base4, 8), 2].reshape(128, 128).astype(F32)
    pp5 = kq[yi, pl.ds(base5, 4), 3].reshape(64, 128).astype(F32)
    pp6 = kq[yi, pl.ds(base6, 2), 4].reshape(32, 128).astype(F32)
    c3 = cl[:, :, CL_AT[0] : CL_AT[1]].reshape(256, 512)
    c4 = cl[pl.ds(base4, 8), :, CL_AT[1] : CL_AT[2]].reshape(128, 768)
    c5 = cl[pl.ds(base5, 4), :, CL_AT[2] : CL_AT[3]].reshape(64, 896)
    c6 = cl[pl.ds(base6, 2), :, CL_AT[3] : CL_AT[4]].reshape(32, 1024)
    first = dot(jnp.concatenate([c3, c4[:, 0:512], c5[:, 0:512], c6[:, 0:512]], axis=0), above2)
    above3 = (pp3 + first[0:256]).astype(BF16)
    second = dot(jnp.concatenate([c4[:, 512:768], c5[:, 512:768], c6[:, 512:768]], axis=0), above3) + first[256:480]
    above4 = (pp4 + second[0:128]).astype(BF16)
    third = dot(jnp.concatenate([c5[:, 768:896], c6[:, 768:896]], axis=0), above4) + second[128:224]
    above5 = (pp5 + third[0:64]).astype(BF16)
    above6 = pp6 + third[64:96] + dot(c6[:, 896:960], above5)
    above6 = above6.astype(BF16)
    k3[...] = above3.reshape(16, 16, 128)
    k4[...] = above4.reshape(8, 16, 128)
    k5[...] = above5.reshape(4, 16, 128)
    k6[...] = above6.reshape(2, 16, 128)
    sv_ref[48:64, :] = k3[zc]
    sv_ref[64:80, :] = k4[near4]
    sv_ref[80:96, :] = k5[near5]
    sv_ref[96:112, :] = k6[near6]

    by_core(wait_opposite)
    for block in range(3):
        @pl.when((block + NX - x) % NX == 2)
        def _(block=block):
            acc[...] += dot_t(ancestors(block), cg[block])

    late = jnp.concatenate(
        [k1[...].reshape(1024, 128)[1000:], above2, above3, above4, above5, above6], axis=0
    )
    total = acc[...] + dot_t(late, cg[3])
    live = lax.broadcasted_iota(jnp.int32, (COLS, LEAF), 1) < rows_ref[0]
    out_ref[...] = jnp.where(live, total, 0.0).astype(BF16)
    for finish in drains:
        finish()


def hand_over(values, leaf, values_out, leaf_out):
    leaf_out[...] = leaf[...]
    values_out[...] = values[...]


N_SEMS = 112


def body(sep_q, sep_phi, coupling, leaf_q, leaf_phi, leaf_coupling, leaf_rows):
    vmem = pl.BlockSpec(memory_space=pltpu.VMEM)
    hbm = pl.BlockSpec(memory_space=pl.ANY)
    block = (16, 128)
    scratch = [
        pltpu.VMEM((56, 128), BF16),
        pltpu.VMEM((8, 4064), BF16),
        pltpu.VMEM((128, 128), BF16),
        pltpu.VMEM((128, LEAF), BF16),
        pltpu.VMEM((1, 328704), BF16),
        pltpu.VMEM((CROWS + 8, 128), F32),
        pltpu.VMEM((128, 1024), BF16),
        pltpu.VMEM((128, 1024), F32),
        pltpu.VMEM((LEVELS - 1, 16, 2048), BF16),
        pltpu.VMEM((LEVELS - 2, 16, 1024), BF16),
        pltpu.VMEM((2048, 128), F32),
        pltpu.VMEM((2048, 128), BF16),
        pltpu.VMEM((1024, 128), BF16),
        pltpu.VMEM((NX, 1016, LEAF), BF16),
        pltpu.VMEM((16, 96, 128), BF16),
        pltpu.VMEM((16, 96, 128), BF16),
        pltpu.VMEM((14,) + block, F32),
        pltpu.VMEM((8,) + block, F32),
        pltpu.VMEM((4,) + block, F32),
        pltpu.VMEM((2,) + block, F32),
        pltpu.VMEM(block, F32),
        pltpu.VMEM((3, 128, 128), F32),
        pltpu.VMEM((16, 16, CL_AT[-1]), BF16),
    ]
    scratch += [pltpu.VMEM(group + (NC,) + block, BF16) for group in GROUPS[:2]]
    scratch += [pltpu.VMEM((2, 16, 5) + block, BF16)]
    scratch += [pltpu.VMEM((n,) + block, BF16) for n in (16, 8, 4, 2)]
    scratch += [
        pltpu.VMEM((LEVELS - 2, 16, 128), F32),
        pltpu.VMEM((COLS, LEAF), F32),
        pltpu.SemaphoreType.DMA((N_SEMS,)),
    ]
    values, leaf = pl.pallas_call(
        kernel,
        out_shape=(
            jax.ShapeDtypeStruct((16 * LEVELS, COLS), BF16),
            jax.ShapeDtypeStruct((COLS, LEAF), BF16),
        ),
        in_specs=[hbm, hbm, hbm, hbm, hbm, hbm, pl.BlockSpec(memory_space=pltpu.SMEM)],
        out_specs=(vmem, vmem),
        scratch_shapes=scratch,
        compiler_params=pltpu.CompilerParams(
            collective_id=0, has_side_effects=True, vmem_limit_bytes=56 * 1024 * 1024
        ),
        cost_estimate=pl.CostEstimate(flops=2_000_000_000, bytes_accessed=4_000_000, transcendentals=0),
    )(sep_q[0].T, sep_phi[0], coupling, leaf_q[0], leaf_phi[0], leaf_coupling[0], leaf_rows)
    values, leaf = pl.pallas_call(
        hand_over,
        out_shape=(
            jax.ShapeDtypeStruct((16 * LEVELS, COLS), BF16),
            jax.ShapeDtypeStruct((COLS, LEAF), BF16),
        ),
        in_specs=[vmem, vmem],
        out_specs=(vmem, vmem),
        compiler_params=pltpu.CompilerParams(vmem_limit_bytes=56 * 1024 * 1024),
    )(values, leaf)
    return values.T[None], leaf[None]


def solution(mesh):
    in_specs = (
        P("sub", "col", None),
        P("sub", None, None),
        P("sub", None),
        P("sub", "col", None),
        P("sub", None, None),
        P("sub", "col", None),
        P("sub"),
    )
    out_specs = (P("sub", "col", None), P("sub", "col", None))
    return jax.shard_map(body, mesh=mesh, in_specs=in_specs, out_specs=out_specs, check_vma=False)
```

time: 73.9 us -> 64.3 us (0.87)
  the two profiles are of different devices: /device:TPU:14 before, /device:TPU:1 now
where the time goes in v2:
time: 64.3 us; the launch traced here: 64.2 us
  Pallas kernels  62.9 us (98%)
  between operations  1.29 us (2%)
    pallas_call x1, Pallas kernels, body(): pl.pallas_call(kernel, out_shape=(jax.ShapeDtypeStruct((16 * LEVELS, COLS...  61.2 us
    pallas_call x1, Pallas kernels, body(): pl.pallas_call(hand_over, out_shape=(jax.ShapeDtypeStruct((16 * LEVELS, C...  1.62 us

profile of v2, /device:TPU:1, one launch (start us, length us, event | category | flops | bytes accessed | tf_op | source)
XLA Modules:
  0.0 64.2 jit_solution(16497169683285033014)
XLA Ops:
  1.3 61.2 %shard_map.86 = (bf16[112,128]{1,0:T(8,128)(2,1)}, bf16[128,640]{1,0:T(8,128)(2,1)}) custom-call(bf16[56,128]{1,0:T(8,128)(2,1)} %bitcast.17, bf16[8,4064]{1,0:T(8,128)(2,1)} %bitcast.14, bf16[1,328704]{1,0:T(2,128)(2,1)} %c_hbm.1, bf16[128,128]{1,0:T(8,128)(2,1)} %bitcast.15, bf16[128,640]{1,0:T(8,128)(2,1)} %bitcast.12, bf16[1016,640]{1,0:T(8,128)(2,1)} %bitcast.11, ...), custom_call_target="tpu_custom_call" | custom-call | flops 2000000000 | bytes 4000000 | tf_op jit(solution)/shard_map/pallas_call | solution.py:554
  62.5 1.6 %shard_map.87 = (bf16[112,128]{1,0:T(8,128)(2,1)}, bf16[128,640]{1,0:T(8,128)(2,1)}) custom-call(bf16[112,128]{1,0:T(8,128)(2,1)} %get-tuple-element.6.values, bf16[128,640]{1,0:T(8,128)(2,1)} %get-tuple-element.7.leaf), custom_call_target="tpu_custom_call" | custom-call | tf_op jit(solution)/shard_map/pallas_call | solution.py:568

commit v3 on v2

--- a/solution.py
+++ b/solution.py
@@ -71,8 +71,9 @@
         new_sems(6),
     ):
         fetches.append(pltpu.make_async_copy(src, dst, sem))
-        fetches[-1].start()
     q_copy, phi_copy, c_copy, cpl_copy, lq_copy, lphi_copy = fetches
+    q_copy.start()
+    phi_copy.start()
 
     barrier = pltpu.get_barrier_semaphore()
     for k in range(1, 16):
@@ -89,6 +90,9 @@
         pl.semaphore_signal(barrier, inc=1, device_id=dev(4 - half + k, z, c), device_id_type=MESH)
     for k in (1, NX - 1):
         pl.semaphore_signal(barrier, inc=1, device_id=(sub, (x + k) % NX), device_id_type=MESH)
+
+    for fetch in (c_copy, cpl_copy, lq_copy, lphi_copy):
+        fetch.start()
 
     q_copy.wait()
     phi_copy.wait()
@@ -121,6 +125,46 @@
 
     pl.semaphore_wait(barrier, 15 + 24 + 8 + 4 + 2)
 
+    lanes = (pl.ds(0, 384), pl.ds(384, 256))
+    left, right = (x + NX - 1) % NX, (x + 1) % NX
+    (gr_send, gl_send, fr_send, fl_send, l0, l1, r0, r1, o_l, o_r) = new_sems(10)
+
+    def by_core(step):
+        for core in range(NC):
+            @pl.when(c == core)
+            def _(core=core):
+                step(lanes[core], lanes[1 - core])
+
+    def give(one, two):
+        for part, rs_right in ((one, l0), (two, l1)):
+            send(cpl_hbm.at[:, part], cg.at[x, :, part], gr_send, rs_right, (sub, right))
+        for part, rs_left in ((two, r0), (one, r1)):
+            send(cpl_hbm.at[:, part], cg.at[x, :, part], gl_send, rs_left, (sub, left))
+
+    def pass_on(one, two):
+        piece = cg.at[left, :, one]
+        drain(piece, l0)
+        send(piece, piece, fr_send, o_l, (sub, right))
+        piece = cg.at[right, :, two]
+        drain(piece, r0)
+        send(piece, piece, fl_send, o_r, (sub, left))
+
+    def wait_neighbours(one, two):
+        drain(cg.at[0, :, two], l1)
+        drain(cg.at[0, :, one], r1)
+
+    def wait_opposite(one, two):
+        drain(cg.at[0, :, one], o_l)
+        drain(cg.at[0, :, two], o_r)
+
+    def finish_gather(one, two):
+        drain(cg.at[0], gr_send)
+        drain(cg.at[0], gl_send)
+        drain(cg.at[0, :, one], fr_send)
+        drain(cg.at[0, :, two], fl_send)
+
+    by_core(give)
+
     base4, base5, base6 = zc - zq, zc - zc % 4, zc - c
     near4, near5, near6 = zq, zc % 4, c
     classes = (
@@ -148,47 +192,6 @@
         return ms.at[d, pl.ds(0, 48 + 16 * n)], mr.at[zc, pl.ds(0, 48 + 16 * n)]
 
     wait_factors = to_row(factors, lambda n, count: mr.at[pl.ds(0, count), pl.ds(0, 48 + 16 * n)])
-
-    lanes = (pl.ds(0, 384), pl.ds(384, 256))
-    left, right = (x + NX - 1) % NX, (x + 1) % NX
-    (gr_send, gl_send, fr_send, fl_send, l0, l1, r0, r1, o_l, o_r) = new_sems(10)
-
-    def by_core(step):
-        for core in range(NC):
-            @pl.when(c == core)
-            def _(core=core):
-                step(lanes[core], lanes[1 - core])
-
-    def give(one, two):
-        for part, rs_right in ((one, l0), (two, l1)):
-            send(cpl_hbm.at[:, part], cg.at[x, :, part], gr_send, rs_right, (sub, right))
-        for part, rs_left in ((two, r0), (one, r1)):
-            send(cpl_hbm.at[:, part], cg.at[x, :, part], gl_send, rs_left, (sub, left))
-
-    def pass_on(one, two):
-        piece = cg.at[left, :, one]
-        drain(piece, l0)
-        send(piece, piece, fr_send, o_l, (sub, right))
-        piece = cg.at[right, :, two]
-        drain(piece, r0)
-        send(piece, piece, fl_send, o_r, (sub, left))
-
-    def wait_neighbours(one, two):
-        drain(cg.at[0, :, two], l1)
-        drain(cg.at[0, :, one], r1)
-
-    def wait_opposite(one, two):
-        drain(cg.at[0, :, one], o_l)
-        drain(cg.at[0, :, two], o_r)
-
-    def finish_gather(one, two):
-        drain(cg.at[0], gr_send)
-        drain(cg.at[0], gl_send)
-        drain(cg.at[0, :, one], fr_send)
-        drain(cg.at[0, :, two], fl_send)
-
-    by_core(give)
-    drains.append(lambda: by_core(finish_gather))
 
     c_copy.wait()
     wide_row = lax.broadcasted_iota(jnp.int32, (128, 1024), 0)
@@ -438,6 +441,10 @@
     drain(br2.at[0], b2_recv)
     product = dot(ct1[...].reshape(80, 1024), kp1[...]) + pv[...].reshape(80, 128)
 
+    def flush(keep):
+        while len(drains) > keep:
+            drains.pop(0)()
+
     def own_rows(s, at):
         return m456[s - 4, pl.ds(pl.multiple_of(at, 16), 16), :]
 
@@ -459,6 +466,8 @@
             @pl.when((block + NX - x) % NX != 2)
             def _(block=block):
                 acc[...] += dot_t(ancestors(block), cg[block])
+
+        flush(1)
 
     spread_pair(during_2)
 
@@ -490,20 +499,25 @@
     sv_ref[80:96, :] = k5[near5]
     sv_ref[96:112, :] = k6[near6]
 
-    by_core(wait_opposite)
-    for block in range(3):
-        @pl.when((block + NX - x) % NX == 2)
-        def _(block=block):
-            acc[...] += dot_t(ancestors(block), cg[block])
-
     late = jnp.concatenate(
         [k1[...].reshape(1024, 128)[1000:], above2, above3, above4, above5, above6], axis=0
     )
-    total = acc[...] + dot_t(late, cg[3])
+
+    @pl.when(x != 1)
+    def _():
+        acc[...] += dot_t(late, cg[3])
+
+    flush(0)
+    by_core(wait_opposite)
+    by_core(finish_gather)
+    for block in range(NX):
+        @pl.when((block + NX - x) % NX == 2)
+        def _(block=block):
+            acc[...] += dot_t(late if block == 3 else ancestors(block), cg[block])
+
+    total = acc[...]
     live = lax.broadcasted_iota(jnp.int32, (COLS, LEAF), 1) < rows_ref[0]
     out_ref[...] = jnp.where(live, total, 0.0).astype(BF16)
-    for finish in drains:
-        finish()
 
 
 def hand_over(values, leaf, values_out, leaf_out):

time: 64.3 us -> 64.3 us (level)
  no operation moved by 1% of the time
where the time goes in v3:
time: 64.3 us; the launch traced here: 64.1 us
  Pallas kernels  62.8 us (98%)
  between operations  1.29 us (2%)
    pallas_call x1, Pallas kernels, body(): pl.pallas_call(kernel, out_shape=(jax.ShapeDtypeStruct((16 * LEVELS, COLS...  61.2 us
    pallas_call x1, Pallas kernels, body(): pl.pallas_call(hand_over, out_shape=(jax.ShapeDtypeStruct((16 * LEVELS, C...  1.62 us

profile of v3, /device:TPU:1, one launch (start us, length us, event | category | flops | bytes accessed | tf_op | source)
XLA Modules:
  0.0 64.1 jit_solution(14386322933017116783)
XLA Ops:
  1.3 61.2 %shard_map.86 = (bf16[112,128]{1,0:T(8,128)(2,1)}, bf16[128,640]{1,0:T(8,128)(2,1)}) custom-call(bf16[56,128]{1,0:T(8,128)(2,1)} %bitcast.17, bf16[8,4064]{1,0:T(8,128)(2,1)} %bitcast.14, bf16[1,328704]{1,0:T(2,128)(2,1)} %c_hbm.1, bf16[128,128]{1,0:T(8,128)(2,1)} %bitcast.15, bf16[128,640]{1,0:T(8,128)(2,1)} %bitcast.12, bf16[1016,640]{1,0:T(8,128)(2,1)} %bitcast.11, ...), custom_call_target="tpu_custom_call" | custom-call | flops 2000000000 | bytes 4000000 | tf_op jit(solution)/shard_map/pallas_call | solution.py:568
  62.5 1.6 %shard_map.87 = (bf16[112,128]{1,0:T(8,128)(2,1)}, bf16[128,640]{1,0:T(8,128)(2,1)}) custom-call(bf16[112,128]{1,0:T(8,128)(2,1)} %get-tuple-element.6.values, bf16[128,640]{1,0:T(8,128)(2,1)} %get-tuple-element.7.leaf), custom_call_target="tpu_custom_call" | custom-call | tf_op jit(solution)/shard_map/pallas_call | solution.py:582

commit v4 on v3

--- a/solution.py
+++ b/solution.py
@@ -263,16 +263,6 @@
 
     wait_lookahead = to_row(lookahead, lambda n, count: cl.at[pl.ds(0, count), :, pl.ds(0, CL_AT[n + 1])])
 
-    quad = mr[pl.ds(base4, 8), 48:64].astype(F32)
-    two = mr[pl.ds(base5, 4), 64:80].astype(F32)
-    chip = mr[pl.ds(base6, 2), 64:96].astype(F32)
-
-    def part(block, at):
-        return block[:, at : at + 8].reshape(-1, 128).astype(BF16)
-
-    m456[0] = dot_t(part(quad, 8), part(quad, 0))
-    m456[1] = dot_t(part(two, 8), part(two, 0))
-    m456[2] = dot_t(part(chip, 8), part(chip, 16))
     arrange(1)
 
     def publish(s, modal):
@@ -415,11 +405,20 @@
 
     def first_0():
         arrange(2)
+        quad = mr[pl.ds(base4, 8), 48:64].astype(F32)
+        two = mr[pl.ds(base5, 4), 64:80].astype(F32)
+        chip = mr[pl.ds(base6, 2), 64:96].astype(F32)
+
+        def part(block, at):
+            return block[:, at : at + 8].reshape(-1, 128).astype(BF16)
+
+        m456[0] = dot_t(part(quad, 8), part(quad, 0))
+        m456[1] = dot_t(part(two, 8), part(two, 0))
+        m456[2] = dot_t(part(chip, 8), part(chip, 16))
+
+    def second_0():
         arrange(3)
-
-    def second_0():
         arrange(4)
-        arrange(5)
         by_core(pass_on)
 
     spread_wide(0, first_0, second_0)
@@ -429,11 +428,9 @@
     publish(1, jnp.sum(br1[...], axis=0) + dot(ct0[0], kp0[...]))
 
     def during_1():
+        arrange(5)
         arrange(6)
         pv[...] = dot(ct0[1:6].reshape(80, 2048), kp0[...]).reshape(5, 16, 128)
-        lq_copy.wait()
-        lphi_copy.wait()
-        acc[...] = dot(lq_ref[...], lphi_ref[...])
 
     spread_half(during_1)
 
@@ -460,6 +457,9 @@
     sv_ref[32:48, :] = blocks[0].astype(BF16)
 
     def during_2():
+        lq_copy.wait()
+        lphi_copy.wait()
+        acc[...] = dot(lq_ref[...], lphi_ref[...])
         cpl_copy.wait()
         by_core(wait_neighbours)
         for block in range(3):

time: 64.3 us -> 64.3 us (level)
  no operation moved by 1% of the time
where the time goes in v4:
time: 64.3 us; the launch traced here: 64.1 us
  Pallas kernels  62.8 us (98%)
  between operations  1.29 us (2%)
    pallas_call x1, Pallas kernels, body(): pl.pallas_call(kernel, out_shape=(jax.ShapeDtypeStruct((16 * LEVELS, COLS...  61.2 us
    pallas_call x1, Pallas kernels, body(): pl.pallas_call(hand_over, out_shape=(jax.ShapeDtypeStruct((16 * LEVELS, C...  1.62 us

profile of v4, /device:TPU:1, one launch (start us, length us, event | category | flops | bytes accessed | tf_op | source)
XLA Modules:
  0.0 64.1 jit_solution(4239002927161952623)
XLA Ops:
  1.3 61.2 %shard_map.86 = (bf16[112,128]{1,0:T(8,128)(2,1)}, bf16[128,640]{1,0:T(8,128)(2,1)}) custom-call(bf16[56,128]{1,0:T(8,128)(2,1)} %bitcast.17, bf16[8,4064]{1,0:T(8,128)(2,1)} %bitcast.14, bf16[1,328704]{1,0:T(2,128)(2,1)} %c_hbm.1, bf16[128,128]{1,0:T(8,128)(2,1)} %bitcast.15, bf16[128,640]{1,0:T(8,128)(2,1)} %bitcast.12, bf16[1016,640]{1,0:T(8,128)(2,1)} %bitcast.11, ...), custom_call_target="tpu_custom_call" | custom-call | flops 2000000000 | bytes 4000000 | tf_op jit(solution)/shard_map/pallas_call | solution.py:568
  62.5 1.6 %shard_map.87 = (bf16[112,128]{1,0:T(8,128)(2,1)}, bf16[128,640]{1,0:T(8,128)(2,1)}) custom-call(bf16[112,128]{1,0:T(8,128)(2,1)} %get-tuple-element.6.values, bf16[128,640]{1,0:T(8,128)(2,1)} %get-tuple-element.7.leaf), custom_call_target="tpu_custom_call" | custom-call | tf_op jit(solution)/shard_map/pallas_call | solution.py:582

commit v5 on v4

--- a/solution.py
+++ b/solution.py
@@ -125,7 +125,7 @@
 
     pl.semaphore_wait(barrier, 15 + 24 + 8 + 4 + 2)
 
-    lanes = (pl.ds(0, 384), pl.ds(384, 256))
+    pieces = (pl.ds(0, 512), pl.ds(512, 504))
     left, right = (x + NX - 1) % NX, (x + 1) % NX
     (gr_send, gl_send, fr_send, fl_send, l0, l1, r0, r1, o_l, o_r) = new_sems(10)
 
@@ -133,35 +133,35 @@
         for core in range(NC):
             @pl.when(c == core)
             def _(core=core):
-                step(lanes[core], lanes[1 - core])
+                step(pieces[core], pieces[1 - core])
 
     def give(one, two):
         for part, rs_right in ((one, l0), (two, l1)):
-            send(cpl_hbm.at[:, part], cg.at[x, :, part], gr_send, rs_right, (sub, right))
+            send(cpl_hbm.at[part], cg.at[x, part], gr_send, rs_right, (sub, right))
         for part, rs_left in ((two, r0), (one, r1)):
-            send(cpl_hbm.at[:, part], cg.at[x, :, part], gl_send, rs_left, (sub, left))
+            send(cpl_hbm.at[part], cg.at[x, part], gl_send, rs_left, (sub, left))
 
     def pass_on(one, two):
-        piece = cg.at[left, :, one]
+        piece = cg.at[left, one]
         drain(piece, l0)
         send(piece, piece, fr_send, o_l, (sub, right))
-        piece = cg.at[right, :, two]
+        piece = cg.at[right, two]
         drain(piece, r0)
         send(piece, piece, fl_send, o_r, (sub, left))
 
     def wait_neighbours(one, two):
-        drain(cg.at[0, :, two], l1)
-        drain(cg.at[0, :, one], r1)
+        drain(cg.at[0, two], l1)
+        drain(cg.at[0, one], r1)
 
     def wait_opposite(one, two):
-        drain(cg.at[0, :, one], o_l)
-        drain(cg.at[0, :, two], o_r)
+        drain(cg.at[0, one], o_l)
+        drain(cg.at[0, two], o_r)
 
     def finish_gather(one, two):
         drain(cg.at[0], gr_send)
         drain(cg.at[0], gl_send)
-        drain(cg.at[0, :, one], fr_send)
-        drain(cg.at[0, :, two], fl_send)
+        drain(cg.at[0, one], fr_send)
+        drain(cg.at[0, two], fl_send)
 
     by_core(give)
 

time: 64.3 us -> 64.3 us (level)
  no operation moved by 1% of the time
where the time goes in v5:
time: 64.3 us; the launch traced here: 64.1 us
  Pallas kernels  62.9 us (98%)
  between operations  1.29 us (2%)
    pallas_call x1, Pallas kernels, body(): pl.pallas_call(kernel, out_shape=(jax.ShapeDtypeStruct((16 * LEVELS, COLS...  61.2 us
    pallas_call x1, Pallas kernels, body(): pl.pallas_call(hand_over, out_shape=(jax.ShapeDtypeStruct((16 * LEVELS, C...  1.62 us

profile of v5, /device:TPU:1, one launch (start us, length us, event | category | flops | bytes accessed | tf_op | source)
XLA Modules:
  0.0 64.1 jit_solution(9747485648697566455)
XLA Ops:
  1.3 61.2 %shard_map.86 = (bf16[112,128]{1,0:T(8,128)(2,1)}, bf16[128,640]{1,0:T(8,128)(2,1)}) custom-call(bf16[56,128]{1,0:T(8,128)(2,1)} %bitcast.17, bf16[8,4064]{1,0:T(8,128)(2,1)} %bitcast.14, bf16[1,328704]{1,0:T(2,128)(2,1)} %c_hbm.1, bf16[128,128]{1,0:T(8,128)(2,1)} %bitcast.15, bf16[128,640]{1,0:T(8,128)(2,1)} %bitcast.12, bf16[1016,640]{1,0:T(8,128)(2,1)} %bitcast.11, ...), custom_call_target="tpu_custom_call" | custom-call | flops 2000000000 | bytes 4000000 | tf_op jit(solution)/shard_map/pallas_call | solution.py:568
  62.5 1.6 %shard_map.87 = (bf16[112,128]{1,0:T(8,128)(2,1)}, bf16[128,640]{1,0:T(8,128)(2,1)}) custom-call(bf16[112,128]{1,0:T(8,128)(2,1)} %get-tuple-element.6.values, bf16[128,640]{1,0:T(8,128)(2,1)} %get-tuple-element.7.leaf), custom_call_target="tpu_custom_call" | custom-call | tf_op jit(solution)/shard_map/pallas_call | solution.py:582

commit v6 on v5

--- a/solution.py
+++ b/solution.py
@@ -419,7 +419,6 @@
     def second_0():
         arrange(3)
         arrange(4)
-        by_core(pass_on)
 
     spread_wide(0, first_0, second_0)
 
@@ -429,6 +428,7 @@
 
     def during_1():
         arrange(5)
+        by_core(pass_on)
         arrange(6)
         pv[...] = dot(ct0[1:6].reshape(80, 2048), kp0[...]).reshape(5, 16, 128)
 

time: 64.3 us -> 64.3 us (level)
  no operation moved by 1% of the time
where the time goes in v6:
time: 64.3 us; the launch traced here: 64.1 us
  Pallas kernels  62.9 us (98%)
  between operations  1.29 us (2%)
    pallas_call x1, Pallas kernels, body(): pl.pallas_call(kernel, out_shape=(jax.ShapeDtypeStruct((16 * LEVELS, COLS...  61.2 us
    pallas_call x1, Pallas kernels, body(): pl.pallas_call(hand_over, out_shape=(jax.ShapeDtypeStruct((16 * LEVELS, C...  1.62 us

profile of v6, /device:TPU:1, one launch (start us, length us, event | category | flops | bytes accessed | tf_op | source)
XLA Modules:
  0.0 64.1 jit_solution(2249811990968211761)
XLA Ops:
  1.3 61.2 %shard_map.86 = (bf16[112,128]{1,0:T(8,128)(2,1)}, bf16[128,640]{1,0:T(8,128)(2,1)}) custom-call(bf16[56,128]{1,0:T(8,128)(2,1)} %bitcast.17, bf16[8,4064]{1,0:T(8,128)(2,1)} %bitcast.14, bf16[1,328704]{1,0:T(2,128)(2,1)} %c_hbm.1, bf16[128,128]{1,0:T(8,128)(2,1)} %bitcast.15, bf16[128,640]{1,0:T(8,128)(2,1)} %bitcast.12, bf16[1016,640]{1,0:T(8,128)(2,1)} %bitcast.11, ...), custom_call_target="tpu_custom_call" | custom-call | flops 2000000000 | bytes 4000000 | tf_op jit(solution)/shard_map/pallas_call | solution.py:568
  62.5 1.6 %shard_map.87 = (bf16[112,128]{1,0:T(8,128)(2,1)}, bf16[128,640]{1,0:T(8,128)(2,1)}) custom-call(bf16[112,128]{1,0:T(8,128)(2,1)} %get-tuple-element.6.values, bf16[128,640]{1,0:T(8,128)(2,1)} %get-tuple-element.7.leaf), custom_call_target="tpu_custom_call" | custom-call | tf_op jit(solution)/shard_map/pallas_call | solution.py:582
